TPU v7x, 256 devices: a whole 4x4x8 slice. The times are simulated.
256 devices in a mesh: row: 32 (over x, z), col: 8 (over y, core).
Axes of the slice: x: 4, y: 4, z: 8, core: 2. Of those that a mesh axis runs over, the one named last changes fastest.
Arguments:
- features: bfloat16 [65536, 128], P(('col', 'row')), may hold values from -6 to 6
- node_ids: int32 [256, 256], P(('col', 'row')), may hold values from 0 to 255, each once within a row
- edge_blocks: bfloat16 [64, 128, 128], replicated, may hold values from -0.25 to 0.25
- block_rows: int32 [32, 8, 256], P('row', 'col'), may hold values from 0 to 15
- block_cols: int32 [32, 8, 256], P('row', 'col'), may hold values from 0 to 63
- block_ids: int32 [32, 8, 256], P('row', 'col'), may hold values from 0 to 63
- live_blocks: int32 [32, 8], P('row', 'col'), may hold values from 1 to 256, as said below
- weight: bfloat16 [128, 256], replicated, may hold values from -0.5 to 0.5
- bias: float32 [256], replicated, may hold values from -4 to 4
- cotangent: bfloat16 [65536, 256], P(('row', 'col')), may hold values from -6 to 6
Outputs:
- layer_out: float32 [65536, 256], P(('row', 'col'))
- feature_grad: float32 [65536, 128], P(('col', 'row'))
- weight_grad: float32 [128, 256], replicated
- bias_grad: float32 [256], replicated
Inputs may be any that keep to these rules, and one draw needn't show every extreme that they name: Only the first live_blocks[r, c] slots of grid cell (r, c) hold blocks; some grid cell uses all 256 slots in every draw.
All inputs are finite; a program needn't handle non-finite values.
Results may differ from a plain program's by a relative error of at most 0.0003.
Values may be sent and summed in bfloat16 or wider, within the bound.
A program may use at most 128 MiB of HBM per device.

v0:
```python
import math

import jax
import jax.numpy as jnp
from jax import lax
from jax.sharding import PartitionSpec as P


def block_sum(
    strip_rows, slot_rows, slot_cols, slot_ids, live_count, edge_blocks, out_count, transpose
):
    highest = lax.Precision.HIGHEST
    blocksize = edge_blocks.shape[1]
    columns_count = strip_rows.shape[1]
    sources = strip_rows.reshape(-1, blocksize, columns_count)
    group_size = 32
    turns = (live_count + group_size - 1) // group_size
    positions = jnp.arange(group_size, dtype=jnp.int32)
    targets = jnp.arange(out_count, dtype=jnp.int32)
    is_wide = strip_rows.dtype == jnp.float32
    pattern = "gji,gjw->giw" if transpose else "gij,gjw->giw"

    def accumulate(turn_index, totals):
        offset = turn_index * group_size
        rows_now = lax.dynamic_slice_in_dim(slot_rows, offset, group_size)
        cols_now = lax.dynamic_slice_in_dim(slot_cols, offset, group_size)
        ids_now = lax.dynamic_slice_in_dim(slot_ids, offset, group_size)
        if transpose:
            picked = sources[rows_now]
            destination = cols_now
        else:
            picked = sources[cols_now]
            destination = rows_now
        weight_tiles = edge_blocks[ids_now]
        if is_wide:
            product = jnp.einsum(
                pattern,
                weight_tiles.astype(jnp.float32),
                picked,
                precision=highest,
                preferred_element_type=jnp.float32,
            )
        else:
            product = jnp.einsum(pattern, weight_tiles, picked, preferred_element_type=jnp.float32)
        in_use = offset + positions < live_count
        selector = ((destination[None, :] == targets[:, None]) & in_use[None, :]).astype(
            jnp.float32
        )
        return totals + jnp.einsum("og,giw->oiw", selector, product, precision=highest)

    start_totals = jnp.zeros((out_count, blocksize, columns_count), jnp.float32)
    totals = lax.fori_loop(0, turns, accumulate, start_totals)
    return totals.reshape(out_count * blocksize, columns_count)


def body(
    features,
    node_ids,
    edge_blocks,
    block_rows,
    block_cols,
    block_ids,
    live_blocks,
    weight,
    bias,
    cotangent,
):
    highest = lax.Precision.HIGHEST
    row_count = lax.axis_size("row")
    col_count = lax.axis_size("col")
    tile_rows = features.shape[0]
    blocksize = edge_blocks.shape[1]
    per_device = tile_rows // blocksize
    slot_rows = block_rows.reshape(-1)
    slot_cols = block_cols.reshape(-1)
    slot_ids = block_ids.reshape(-1)
    live_count = live_blocks.reshape(-1)[0]
    local_ids = node_ids.reshape(-1)
    ordered = features[local_ids]
    weight_wide = weight.astype(jnp.float32)
    cotangent_wide = cotangent.astype(jnp.float32)
    scale_factor = 1.0 / math.sqrt(tile_rows * row_count * col_count)
    transformed = jnp.dot(ordered, weight, preferred_element_type=jnp.float32)
    column_strip = lax.all_gather(transformed, "row", axis=0, tiled=True)
    partials = block_sum(
        column_strip,
        slot_rows,
        slot_cols,
        slot_ids,
        live_count,
        edge_blocks,
        per_device * col_count,
        False,
    )
    layer_out = lax.psum_scatter(partials, "col", scatter_dimension=0, tiled=True) + bias
    row_strip = lax.all_gather(cotangent, "col", axis=0, tiled=True)
    transposed = block_sum(
        row_strip,
        slot_rows,
        slot_cols,
        slot_ids,
        live_count,
        edge_blocks,
        per_device * row_count,
        True,
    )
    pulled_back = lax.psum_scatter(transposed, "row", scatter_dimension=0, tiled=True)
    grad_ordered = jnp.dot(pulled_back, weight_wide.T, precision=highest)
    weight_term = jnp.dot(ordered.astype(jnp.float32).T, pulled_back, precision=highest)
    bias_term = jnp.sum(cotangent_wide, axis=0)
    weight_grad, bias_grad = lax.psum(
        (weight_term * scale_factor, bias_term * scale_factor), ("row", "col")
    )
    feature_grad = jnp.zeros_like(grad_ordered).at[local_ids].set(grad_ordered)
    return (layer_out, feature_grad, weight_grad, bias_grad)


def solution(mesh):
    return jax.shard_map(
        body,
        mesh=mesh,
        in_specs=(
            P(("col", "row"), None),
            P(("col", "row"), None),
            P(),
            P("row", "col", None),
            P("row", "col", None),
            P("row", "col", None),
            P("row", "col"),
            P(),
            P(),
            P(("row", "col"), None),
        ),
        out_specs=(P(("row", "col"), None), P(("col", "row"), None), P(), P()),
        check_vma=False,
    )
```

profile of v0, /device:TPU:1, one launch (start us, length us, event | category | flops | bytes accessed | tf_op | source)
XLA Modules:
  0.0 694.1 jit_solution(10249959226075010375)
XLA Ops:
  11.9 28.2 %all-gather.5.cloned.1.call-done = bf16[2048,256]{1,0:T(8,128)(2,1)} async-done(((bf16[256,256]{1,0:T(8,128)(2,1)}), bf16[2048,256]{1,0:T(8,128)(2,1)}) %all-gather.5.cloned.1.call-update) | async-done | bytes 1048592 | tf_op jit(solution)/shard_map/all_gather | solution.py:96
  40.1 4.3 broadcast_in_dim.32
  44.4 29.6 %while.23 = (s32[]{:T(128)}, f32[64,128,256]{2,0,1:T(8,128)}, s32[]{:T(128)}, s32[256]{0:T(256)S(1)}, s32[]{:T(128)}, /*index=5*/s32[256]{0:T(256)S(1)}, bf16[64...) while((s32[]{:T(128)}, f32[64,128,256]{2,0,1:T(8,128)}, ...), condition=%wide.region_4.5_spmd.clone, body=%wide.region_3.4_spmd.clone.sunk | while | flops 1075845376 | bytes 38807196 | solution.py:52
  45.2 2.3 gather_fusion.2
  49.0 10.1 %fusion.73 = f32[64,128,256]{2,0,1:T(8,128)} fusion(f32[64,128,256]{2,0,1:T(8,128)} %get-tuple-element.379, f32[32,128,256]{2,1,0:T(8,128)S(1)} %fusion.71, s32[32]{0:T(128)S(1)} %dynamic_slice.35, pred[32]{0:T(512)(128)(4,1)S(1)} %fusion.72), kind=kOutput, calls=%fused_computation.26.clone.1 | convolution fusion | flops 807407616 | bytes 20971680 | tf_op jit(solution)/shard_map/while/body/og,giw->oiw/dot_general | solution.py:49
  60.0 2.3 gather_fusion.2
  63.8 10.2 %fusion.73 = f32[64,128,256]{2,0,1:T(8,128)} fusion(f32[64,128,256]{2,0,1:T(8,128)} %get-tuple-element.379, f32[32,128,256]{2,1,0:T(8,128)S(1)} %fusion.71, s32[32]{0:T(128)S(1)} %dynamic_slice.35, pred[32]{0:T(512)(128)(4,1)S(1)} %fusion.72), kind=kOutput, calls=%fused_computation.26.clone.1 | convolution fusion | flops 807407616 | bytes 20971680 | tf_op jit(solution)/shard_map/while/body/og,giw->oiw/dot_general | solution.py:49
  74.0 11.5 %copy.16 = f32[64,128,256]{2,1,0:T(8,128)} copy(f32[64,128,256]{2,0,1:T(8,128)} %get-tuple-element.415) | data formatting | bytes 16777216 | tf_op jit(solution)/shard_map/while | solution.py:52
  85.6 55.0 %all-gather.3.cloned.1.call-done = f32[8192,256]{1,0:T(8,128)} async-done(((f32[256,256]{1,0:T(8,128)}), f32[8192,256]{1,0:T(8,128)}) %all-gather.3.cloned.1.call-update) | async-done | bytes 8388624 | tf_op jit(solution)/shard_map/all_gather | solution.py:84
  140.8 37.3 %while.22 = (s32[]{:T(128)}, f32[16,128,256]{2,0,1:T(8,128)S(1)}, s32[]{:T(128)}, s32[256]{0:T(256)S(1)}, s32[]{:T(128)}, /*index=5*/s32[256]{0:T(256)S(1)}, bf1...) while((s32[]{:T(128)}, f32[16,128,256]{2,0,1:T(8,128)S(1)}, ...), condition=%wide.region_1.2_spmd.clone, body=%wide.region_0.1_spmd.clone.sunk | while | flops 1812466944 | bytes 28321404 | solution.py:52
  141.1 6.1 gather_fusion.1
  147.3 2.3 gather_fusion
  149.6 4.5 fusion.64
  154.8 4.7 fusion.66
  159.7 6.1 gather_fusion.1
  165.8 2.3 gather_fusion
  168.2 4.5 fusion.64
  173.4 4.7 fusion.66
  178.2 2.6 copy.15
  180.9 222.0 %psum.15 = f32[256]{0:T(256)} all-reduce(f32[256]{0:T(256)S(1)} %broadcast_multiply_fusion), channel_id=1, replica_groups=mesh['row'=32,'col'=8] {'row','col'}, use_global_device_ids=true, to_apply=%region_9.10 | all-reduce | flops 256 | bytes 2048 | tf_op jit(solution)/shard_map/psum | solution.py:111
  404.1 1.8 scatter_custom_fusion
  405.8 1.9 convolution_multiply_fusion
  407.7 29.3 %reduce-scatter.3.cloned.1.call-done = f32[256,256]{1,0:T(8,128)} async-done(((f32[2048,256]{1,0:T(8,128)}), f32[256,256]{1,0:T(8,128)}) %reduce-scatter.3.cloned.1.call-update) | async-done | bytes 262160 | tf_op jit(solution)/shard_map/reduce_scatter | solution.py:95
  438.7 247.3 %all-reduce.2.cloned.1.call-done = f32[128,256]{1,0:T(8,128)} async-done(((f32[128,256]{1,0:T(8,128)}), f32[128,256]{1,0:T(8,128)}) %all-reduce.2.cloned.1.call-update) | async-done | bytes 131088 | tf_op jit(solution)/shard_map/psum | solution.py:111
  (63 shorter events, 15.1 us)
Async XLA Ops:
  7.2 3.1 copy-start
  7.2 32.9 %all-gather.5.cloned.1.call-start = ((), (), s32[]{:S(2)}) async-start(), calls=%async_computation.4 | async-start | bytes 1179648 | tf_op jit(solution)/shard_map/all_gather | solution.py:96
  7.9 132.7 %all-gather.3.cloned.1.call-start = ((), (), s32[]{:S(2)}) async-start(), calls=%async_computation.2 | async-start | bytes 8650752 | tf_op jit(solution)/shard_map/all_gather | solution.py:84
  11.1 391.7 %reduce-scatter.5.cloned.1.call-start = ((), (), s32[]{:S(2)}) async-start(), calls=%async_computation.5 | async-start | bytes 8650752 | tf_op jit(solution)/shard_map/reduce_scatter | solution.py:107
  40.1 4.3 copy-start.1
  40.1 4.3 copy-start.4
  40.1 4.3 copy-start.5
  40.1 4.3 copy-start.6
  49.0 10.2 %copy-start.2 = (bf16[2048,256]{1,0:T(8,128)(2,1)S(1)}, bf16[2048,256]{1,0:T(8,128)(2,1)}, u32[]{:S(2)}) copy-start(bf16[2048,256]{1,0:T(8,128)(2,1)} %get-tuple-element.427) | copy-start | bytes 3145732 | tf_op jit(solution)/shard_map/while
  63.8 10.2 %copy-start.2 = (bf16[2048,256]{1,0:T(8,128)(2,1)S(1)}, bf16[2048,256]{1,0:T(8,128)(2,1)}, u32[]{:S(2)}) copy-start(bf16[2048,256]{1,0:T(8,128)(2,1)} %get-tuple-element.427) | copy-start | bytes 3145732 | tf_op jit(solution)/shard_map/while
  85.5 351.5 %reduce-scatter.3.cloned.1.call-start = ((), (), s32[]{:S(2)}) async-start(), calls=%async_computation.3 | async-start | bytes 2359296 | tf_op jit(solution)/shard_map/reduce_scatter | solution.py:95
  178.1 2.7 copy-start.3
  178.2 258.9 %copy-start.7 = (f32[256]{0:T(256)S(1)}, f32[256]{0:T(256)}, u32[]{:S(2)}) copy-start(f32[256]{0:T(256)} %param.22) | copy-start | bytes 3076
  180.7 505.3 %all-reduce.2.cloned.1.call-start = ((), (), s32[]{:S(2)}) async-start(), calls=%async_computation.6 | async-start | bytes 262144 | tf_op jit(solution)/shard_map/psum | solution.py:111
Sparse Core Ops, SparseCore 0:
  9.9 30.1 all-gather.4
  43.2 97.2 all-gather.2
  144.6 253.8 reduce-scatter.4
  401.0 35.9 reduce-scatter.2
  443.9 242.1 all-reduce.1
where the time goes:
time: 696 us; the launch traced here: 694 us
  waiting for transfers between devices  361 us (52%)
  blocking collectives  222 us (32%)
  local copies, waits for them, and re-layouts  46.9 us (7%)
  matrix products  44.2 us (6%)
  between operations  14.5 us (2%)
    psum x1, waiting for transfers between devices, body(): lax.psum((weight_term * scale_factor, bias_term * scale_factor), ('row',...  247 us
    psum x1, blocking collectives, body(): lax.psum((weight_term * scale_factor, bias_term * scale_factor), ('row',...  222 us
    all_gather x1, waiting for transfers between devices, body(): column_strip = lax.all_gather(transformed, 'row', axis=0, tiled=True)  55 us
    dot_general x4, matrix products, accumulate(): jnp.einsum('og,giw->oiw', selector, product, precision=highest)  29.8 us
    reduce_scatter x1, waiting for transfers between devices, body(): lax.psum_scatter(partials, 'col', scatter_dimension=0, tiled=True) + bias  29.3 us
    all_gather x1, waiting for transfers between devices, body(): row_strip = lax.all_gather(cotangent, 'col', axis=0, tiled=True)  28.2 us
    while x2, local copies, waits for them, and re-layouts, block_sum(): totals = lax.fori_loop(0, turns, accumulate, start_totals)  14.1 us
  transfers between devices with their start and end apart: 5, of which 4 were waited for; matrix products, arithmetic and copies ran while one was open for 14% of the time, Pallas kernels for 0%

commit v1 on v0

v1 whole, which is shorter than its diff:
```python
import functools
import math

import jax
import jax.numpy as jnp
from jax import lax
from jax.experimental import pallas as pl
from jax.experimental.pallas import tpu as pltpu
from jax.sharding import PartitionSpec as P

F32 = jnp.float32
BF16 = jnp.bfloat16
MESH = pl.DeviceIdType.MESH

NX, NZ, NY, NCORE = 4, 8, 4, 2
NROW, NCOL = NX * NZ, NY * NCORE
BLK = 128
SLOTS = 256
FPAIRS = (SLOTS + 2 * NCOL) // 2
BPAIRS = (SLOTS + 2 * NROW) // 2
QLEN = 384


def iota(shape, dim):
    return lax.broadcasted_iota(jnp.int32, shape, dim).astype(F32)


def to_column(row, size):
    eye = iota((size, size), 0) == iota((size, size), 1)
    return jnp.sum(jnp.where(eye, row, 0.0), axis=1, keepdims=True)


def sort_direction(key, code, live, zero_source, empty_pair, keep_out):
    lane = iota((1, SLOTS), 1)
    key = jnp.where(lane < live, key, 1000.0)
    key_col = to_column(key, SLOTS)
    code_col = to_column(code, SLOTS)
    earlier = iota((SLOTS, SLOTS), 1) < iota((SLOTS, SLOTS), 0)
    same = jnp.where((key_col == key) & earlier, 1.0, 0.0)
    rank = jnp.sum(same, axis=1, keepdims=True)
    names = iota((SLOTS, 128), 1)
    count = jnp.sum(jnp.where(key_col == names, 1.0, 0.0), axis=0, keepdims=True)
    padded = 2.0 * jnp.floor((count + 1.0) * 0.5)
    before = jnp.sum(jnp.where(names < key_col, padded, 0.0), axis=1, keepdims=True)
    place = jnp.where(key_col < 999.0, before + rank, -1.0)
    spot = iota((SLOTS, QLEN), 1)
    picked = jnp.sum(jnp.where(place == spot, code_col, 0.0), axis=0, keepdims=True)
    picked = picked.astype(jnp.int32)
    empty = picked == 0
    ids = jnp.where(empty, 0, lax.shift_right_logical(picked - 1, 7))
    src = jnp.where(empty, zero_source, (picked - 1) & 127)
    padded_col = to_column(padded, 128)
    count_col = to_column(count, 128)
    upper = iota((128, 128), 0) < iota((128, 128), 1)
    offset = jnp.sum(jnp.where(upper, padded_col, 0.0), axis=0, keepdims=True)
    ends = jnp.where(count > 0.0, (offset + padded) * 0.5 - 1.0, float(empty_pair))
    offset_col = to_column(offset, 128)
    start_col = jnp.where(count_col > 0.0, offset_col * 0.5, -1.0)
    starts = jnp.sum(jnp.where(start_col == iota((128, QLEN), 1), 1.0, 0.0), axis=0, keepdims=True)
    keep = 1.0 - starts
    return ids, src, keep.astype(jnp.int32), ends.astype(jnp.int32)


def prep_kernel(rows_ref, cols_ref, ids_ref, live_ref, out_ref):
    live = live_ref[0, 0].astype(F32)
    rows = rows_ref[...].reshape(1, SLOTS)
    cols = cols_ref[...].reshape(1, SLOTS)
    ids = ids_ref[...].reshape(1, SLOTS)
    half = cols & 1
    dev = lax.shift_right_logical(cols, 1)
    dev_x = lax.shift_right_logical(dev, 3)
    dev_z = dev & 7
    at_a = dev_z * NX + dev_x
    where_x = jnp.where(half == 0, at_a, dev + NROW)
    f = sort_direction(
        rows.astype(F32), (ids * 128 + where_x + 1).astype(F32), live, 2 * NROW, FPAIRS, None
    )
    b = sort_direction(
        cols.astype(F32), (ids * 128 + rows + 1).astype(F32), live, 2 * NCOL, BPAIRS, None
    )
    out_ref[...] = jnp.zeros((8, QLEN), jnp.int32)
    for k in range(3):
        out_ref[k : k + 1, :] = f[k]
        out_ref[3 + k : 4 + k, :] = b[k]
    out_ref[6:7, 0:128] = f[3]
    out_ref[7:8, 0:128] = b[3]


class Counter:
    def __init__(self):
        self.n = 0

    def take(self, *dims):
        base = self.n
        self.n += math.prod(dims)

        def at(*index):
            k = 0
            for d, i in zip(dims, index):
                assert 0 <= i < d
                k = k * d + i
            return base + k

        return at


def semaphores():
    c = Counter()
    names = dict(
        ax=(4,), ar=(5, 4), al=(4, 4), br=(5,), bl=(4,), bx=(8, 4),
        cy=(4,), cs=(4,),
        ra=(4, 4), la=(3, 4), xa=(4,), rb=(4,), lb=(3,), xb=(8, 4),
        ys=(4,), yy=(4,), w1=(8,), w2=(4,), w3=(8,), w4=(4,), w5=(8,),
    )
    return {k: c.take(*d) for k, d in names.items()}, c.n


SEM, NSEM = semaphores()


def split(value):
    high = value.astype(BF16)
    low = (value - high.astype(F32)).astype(BF16)
    return high, low


def dot(a, b):
    return jnp.dot(a, b, preferred_element_type=F32)


def main_kernel(
    idx, feat, nid, edge, weight, bias, cot,
    out_ref, fg_ref, wg_ref, bg_ref,
    xs, cs, et, phl, sb, sf, ts, yb, ra_r, ra_l, xa_r, rb_r, rb_l, xb_r, ys_r, yy_r,
    wp, w1_r, w2_s, w2_r, w3_r, w4_r, w5_r, ss, rs,
):
    r = lax.axis_index("row")
    c = lax.axis_index("col")
    x, z = r // NZ, lax.rem(r, NZ)
    y, core = c // NCORE, lax.rem(c, NCORE)

    def xm(d):
        return lax.rem(x + d + NX, NX)

    def zm(d):
        return lax.rem(z + d + NZ, NZ)

    def ym(d):
        return lax.rem(y + d + NY, NY)

    def plane(px, pz):
        return (px * NZ + pz, c)

    def column(py, pc):
        return (r, py * NCORE + pc)

    def col_id(d):
        return (r, lax.rem(c + d, NCOL))

    started = []
    pending = {}

    def send(key, src, dst, dev):
        k = SEM[key[0]](*key[1:])
        d = pltpu.make_async_remote_copy(
            src_ref=src, dst_ref=dst, send_sem=ss.at[k], recv_sem=rs.at[k],
            device_id=dev, device_id_type=MESH,
        )
        d.start()
        pending[key] = d
        started.append(d)

    def recv(*key):
        pending.pop(key).wait_recv()

    barrier = pltpu.get_barrier_semaphore()
    peers = [plane(xm(d), z) for d in range(1, NX)]
    peers += [plane(x, zm(d)) for d in range(1, NZ)]
    peers += [col_id(d) for d in range(1, NCOL)]
    for p in peers:
        pl.semaphore_signal(barrier, inc=1, device_id=p, device_id_type=MESH)

    order = jnp.where(
        lax.broadcasted_iota(jnp.int32, (2 * BLK, 2 * BLK), 0) == nid[...], 1.0, 0.0
    )
    order_t = order.T.astype(BF16)
    ordered = dot(order_t, feat[...]).astype(BF16)
    xs[pl.ds(z * NX + x, 1)] = ordered[None, :BLK]
    xs[pl.ds(NROW + r, 1)] = ordered[None, BLK:]
    pl.semaphore_wait(barrier, len(peers))

    def a_at(pz, px):
        return xs.at[pz * NX + px]

    def b_at(px, pz):
        return xs.at[NROW + px * NZ + pz]

    def ag_ar(s, f):
        o = a_at(zm(1 - s), xm(-f))
        send(("ar", s, f), o, o, plane(x, zm(1)))

    def ag_al(s, f):
        o = a_at(zm(s - 1), xm(-f))
        send(("al", s, f), o, o, plane(x, zm(-1)))

    def ag_br(s):
        o = b_at(x, zm(1 - s))
        send(("br", s), o, o, plane(x, zm(1)))

    def ag_bl(s):
        o = b_at(x, zm(s - 1))
        send(("bl", s), o, o, plane(x, zm(-1)))

    def ag_bx(rel):
        o = b_at(x, zm(-rel))
        for d in range(1, NX):
            send(("bx", rel, d), o, o, plane(xm(d), z))

    mine = cs.at[c]
    for d in range(1, NY):
        send(("cy", d), cot, mine, column(ym(d), core))
    send(("cs", 0), cot, mine, column(y, 1 - core))
    ag_ar(1, 0)
    ag_al(1, 0)
    for d in range(1, NX):
        o = a_at(z, x)
        send(("ax", d), o, o, plane(xm(d), z))
    ag_br(1)
    ag_bl(1)
    ag_bx(0)
    cs[pl.ds(c, 1)] = cot[...][None]

    xs[2 * NROW] = jnp.zeros((BLK, BLK), BF16)
    phl[2 * NCOL] = jnp.zeros((BLK, 2 * BLK), BF16)
    sb[BPAIRS] = jnp.zeros((BLK, BLK), F32)
    sf[FPAIRS] = jnp.zeros((BLK, BLK), F32)

    def turn(k, carry):
        for u in range(4):
            et[4 * k + u] = edge[4 * k + u].T
        return carry

    lax.fori_loop(0, 16, turn, 0)

    for f in range(1, NX):
        recv("ax", f)
        ag_ar(1, f)
        ag_al(1, f)
    for d in range(1, NY):
        recv("cy", d)
        o = cs.at[ym(-d) * NCORE + core]
        send(("cs", d), o, o, column(y, 1 - core))

    def project(k):
        p = lax.dot_general(
            cs[k], weight[...], (((1,), (1,)), ((), ())), preferred_element_type=F32
        )
        high, low = split(p)
        both = jnp.concatenate([high, low], axis=1)
        phl[pl.ds(2 * k, 1)] = both[None, :BLK]
        phl[pl.ds(2 * k + 1, 1)] = both[None, BLK:]

    for d in range(NY):
        project(ym(-d) * NCORE + core)
    for d in range(NY):
        recv("cs", d)
    for d in range(NY):
        project(ym(-d) * NCORE + 1 - core)

    def ag_step(s):
        for f in range(NX):
            recv("ar", s, f)
            if s < 4:
                ag_ar(s + 1, f)
            if s < 4:
                recv("al", s, f)
                if s < 3:
                    ag_al(s + 1, f)
        recv("br", s)
        if s < 4:
            ag_br(s + 1)
        ag_bx(s)
        if s < 4:
            recv("bl", s)
            if s < 3:
                ag_bl(s + 1)
            ag_bx(NZ - s)

    def pair(p, base, table, source, sums, total):
        e0, e1 = idx[base, 2 * p], idx[base, 2 * p + 1]
        s0, s1 = idx[base + 1, 2 * p], idx[base + 1, 2 * p + 1]
        keep = idx[base + 2, p].astype(F32)
        left = jnp.concatenate([table[e0], table[e1]], axis=1)
        right = jnp.concatenate([source[s0], source[s1]], axis=0)
        prod = dot(left, right)
        if prod.shape[1] == 2 * BLK:
            prod = prod[:, :BLK] + prod[:, BLK:]
        total = total * keep + prod
        sums[pl.ds(p, 1)] = total[None]
        return total

    def run_pairs(lo, hi, unroll, total, base, table, source, sums):
        assert (hi - lo) % unroll == 0

        def step(k, total):
            for u in range(unroll):
                total = pair(lo + k * unroll + u, base, table, source, sums, total)
            return total

        return lax.fori_loop(0, (hi - lo) // unroll, step, total)

    zero = jnp.zeros((BLK, BLK), F32)
    ag_step(1)
    total = run_pairs(0, 40, 4, zero, 3, et, phl, sb)
    ag_step(2)
    total = run_pairs(40, 80, 4, total, 3, et, phl, sb)
    ag_step(3)
    total = run_pairs(80, 120, 4, total, 3, et, phl, sb)
    ag_step(4)
    run_pairs(120, 160, 4, total, 3, et, phl, sb)

    def stage(k, carry):
        px, pz = k // NZ, lax.rem(k, NZ)
        ts[pl.ds(pz * NX + px, 1)] = sb[idx[7, 2 * k]][None]
        ts[pl.ds(NROW + k, 1)] = sb[idx[7, 2 * k + 1]][None]
        return carry

    lax.fori_loop(0, NROW, stage, 0)

    def t_a(pz, px):
        return pz * NX + px

    def t_b(px, pz):
        return NROW + px * NZ + pz

    def add(at, *refs):
        v = ts[pl.ds(at, 1)]
        for ref in refs:
            v = v + ref[...][None]
        ts[pl.ds(at, 1)] = v

    def rs_ra(s, f):
        at = t_a(zm(4 - s), xm(f))
        if s:
            recv("ra", s - 1, f)
            add(at, ra_r.at[s - 1, f])
        send(("ra", s, f), ts.at[at], ra_r.at[s, f], plane(x, zm(1)))

    def rs_la(s, f):
        at = t_a(zm(s - 3), xm(f))
        if s:
            recv("la", s - 1, f)
            add(at, ra_l.at[s - 1, f])
        send(("la", s, f), ts.at[at], ra_l.at[s, f], plane(x, zm(-1)))

    def rs_bx(rel):
        for d in range(1, NX):
            at = t_b(xm(d), zm(rel))
            send(("xb", rel, d), ts.at[at], xb_r.at[rel, d - 1], plane(xm(d), z))

    def rs_bg(rel):
        for d in range(1, NX):
            recv("xb", rel, d)
        add(t_b(x, zm(rel)), *[xb_r.at[rel, d - 1] for d in range(1, NX)])

    def rs_rb(s):
        rs_bg((4 - s) % NZ)
        at = t_b(x, zm(4 - s))
        if s:
            recv("rb", s - 1)
            add(at, rb_r.at[s - 1])
        send(("rb", s), ts.at[at], rb_r.at[s], plane(x, zm(1)))

    def rs_lb(s):
        rs_bg((s - 3) % NZ)
        at = t_b(x, zm(s - 3))
        if s:
            recv("lb", s - 1)
            add(at, rb_l.at[s - 1])
        send(("lb", s), ts.at[at], rb_l.at[s], plane(x, zm(-1)))

    for f in range(NX):
        rs_ra(0, f)
        rs_la(0, f)
    for rel in (4, 5, 3, 6, 2, 7, 1, 0):
        rs_bx(rel)

    for rel in range(NZ):
        for d in range(1, NX):
            recv("bx", rel, d)

    total = run_pairs(0, 44, 4, zero, 0, edge, xs, sf)
    for f in range(NX):
        rs_ra(1, f)
        rs_la(1, f)
    rs_rb(0)
    rs_lb(0)
    total = run_pairs(44, 92, 4, total, 0, edge, xs, sf)
    for f in range(NX):
        rs_ra(2, f)
        rs_la(2, f)
    rs_rb(1)
    rs_lb(1)
    run_pairs(92, 136, 4, total, 0, edge, xs, sf)

    def stage_y(k, carry):
        yb[pl.ds(k, 1)] = sf[idx[6, k]][None]
        return carry

    lax.fori_loop(0, 2 * NCOL, stage_y, 0)
    for py in range(NY):
        at = 2 * (py * NCORE + 1 - core)
        send(("ys", py), yb.at[pl.ds(at, 2)], ys_r.at[py], column(y, 1 - core))

    for f in range(NX):
        rs_ra(3, f)
    rs_rb(2)
    rs_lb(2)

    def grad(k, carry):
        acc, low_sum = carry
        strip = cs[k]
        agg = yb[pl.ds(2 * k, 2)].reshape(2 * BLK, BLK)
        high, low = split(agg.T)
        acc = acc + dot(high, strip) + dot(low, strip)
        low_sum = low_sum + dot(jnp.ones((8, 2 * BLK), BF16), strip)
        return acc, low_sum

    acc, low_sum = lax.fori_loop(
        0, NCOL, grad, (jnp.zeros((BLK, 2 * BLK), F32), jnp.zeros((8, 2 * BLK), F32))
    )
    wp[...] = (acc * (1.0 / 256.0)).reshape(NCOL, 16, 2 * BLK)
    for d in range(1, NCOL):
        to = lax.rem(c + d, NCOL)
        send(("w1", d), wp.at[to], w1_r.at[d - 1], col_id(d))

    for f in range(NX):
        recv("ra", 3, f)
        recv("la", 2, f)
        add(t_a(z, xm(f)), ra_r.at[3, f], ra_l.at[2, f])
        if f:
            send(("xa", f), ts.at[t_a(z, xm(f))], xa_r.at[f - 1], plane(xm(f), z))
    rs_rb(3)

    for py in range(NY):
        recv("ys", py)
    for py in range(NY):
        at = 2 * (py * NCORE + core)
        yb[pl.ds(at, 2)] = yb[pl.ds(at, 2)] + ys_r[py]
    for d in range(1, NY):
        at = 2 * (ym(d) * NCORE + core)
        send(("yy", d), yb.at[pl.ds(at, 2)], yy_r.at[d - 1], column(ym(d), core))

    for d in range(1, NCOL):
        recv("w1", d)
    part = wp[c]
    for d in range(1, NCOL):
        part = part + w1_r[d - 1]
    low_row = low_sum[0:1] * (1.0 / 256.0)
    bias_tile = jnp.concatenate(
        [low_row[:, :BLK], low_row[:, BLK:], jnp.zeros((6, BLK), F32)], axis=0
    )
    for t in range(NX):
        a, b = 8 * (t // 2), BLK * (t % 2)
        w2_s[t, 0:8] = part[a : a + 8, b : b + BLK]
        w2_s[t, 8:16] = bias_tile
    w2_r[pl.ds(x, 1)] = w2_s[pl.ds(x, 1)]
    for d in range(1, NX):
        send(("w2", d), w2_s.at[xm(d)], w2_r.at[x], plane(xm(d), z))

    recv("rb", 3)
    recv("lb", 2)
    rs_bg(0)
    add(t_b(x, z), rb_r.at[3], rb_l.at[2])
    for f in range(1, NX):
        recv("xa", f)
    add(t_a(z, x), *[xa_r.at[f - 1] for f in range(1, NX)])

    for d in range(1, NX):
        recv("w2", d)
    w3_r[pl.ds(z, 1)] = (((w2_r[0] + w2_r[1]) + w2_r[2]) + w2_r[3])[None]
    for d in range(1, NZ):
        send(("w3", d), w3_r.at[z], w3_r.at[z], plane(x, zm(d)))

    order_b = order.astype(BF16)
    whole = jnp.concatenate([ts[t_a(z, x)], ts[t_b(x, z)]], axis=0)
    high, low = split(whole)
    fg_ref[...] = dot(order_b, high) + dot(order_b, low)

    for d in range(1, NZ):
        recv("w3", d)
    tile = w3_r[0]
    for k in range(1, NZ):
        tile = tile + w3_r[k]
    w4_r[pl.ds(x, 1)] = tile[None, 0:8]
    for d in range(1, NX):
        send(("w4", d), w4_r.at[x], w4_r.at[x], plane(xm(d), z))
    bg_ref[...] = jnp.concatenate([tile[8:9], tile[9:10]], axis=1)

    for d in range(1, NY):
        recv("yy", d)
    agg = yb[pl.ds(2 * c, 2)]
    for d in range(1, NY):
        agg = agg + yy_r[d - 1]
    high, low = split(agg.reshape(2 * BLK, BLK))
    out_ref[...] = dot(high, weight[...]) + dot(low, weight[...]) + bias[...]

    for d in range(1, NX):
        recv("w4", d)
    w5_r[pl.ds(c, 1)] = w4_r[...][None]
    for d in range(1, NCOL):
        send(("w5", d), w5_r.at[c], w5_r.at[c], col_id(d))
    for d in range(1, NCOL):
        recv("w5", d)
    for k in range(NCOL):
        for t in range(NX):
            a, b = 16 * k + 8 * (t // 2), BLK * (t % 2)
            wg_ref[a : a + 8, b : b + BLK] = w5_r[k, t]

    assert not pending, pending.keys()
    for d in started:
        d.wait_send()


def body(
    features, node_ids, edge_blocks, block_rows, block_cols, block_ids, live_blocks,
    weight, bias, cotangent,
):
    vmem = pl.BlockSpec(memory_space=pltpu.VMEM)
    smem = pl.BlockSpec(memory_space=pltpu.SMEM)
    plan = pl.pallas_call(
        prep_kernel,
        out_shape=jax.ShapeDtypeStruct((8, QLEN), jnp.int32),
        in_specs=[vmem, vmem, vmem, smem],
        out_specs=vmem,
    )(block_rows, block_cols, block_ids, live_blocks)
    tile = (BLK, BLK)
    scratch = [
        pltpu.VMEM((2 * NROW + 1, *tile), BF16),
        pltpu.VMEM((NCOL, 2 * BLK, 2 * BLK), BF16),
        pltpu.VMEM((64, *tile), BF16),
        pltpu.VMEM((2 * NCOL + 1, BLK, 2 * BLK), BF16),
        pltpu.VMEM((BPAIRS + 1, *tile), F32),
        pltpu.VMEM((FPAIRS + 1, *tile), F32),
        pltpu.VMEM((2 * NROW, *tile), F32),
        pltpu.VMEM((2 * NCOL, *tile), F32),
        pltpu.VMEM((4, 4, *tile), F32),
        pltpu.VMEM((3, 4, *tile), F32),
        pltpu.VMEM((3, *tile), F32),
        pltpu.VMEM((4, *tile), F32),
        pltpu.VMEM((3, *tile), F32),
        pltpu.VMEM((8, 3, *tile), F32),
        pltpu.VMEM((4, 2, *tile), F32),
        pltpu.VMEM((3, 2, *tile), F32),
        pltpu.VMEM((NCOL, 16, 2 * BLK), F32),
        pltpu.VMEM((NCOL - 1, 16, 2 * BLK), F32),
        pltpu.VMEM((NX, 16, BLK), F32),
        pltpu.VMEM((NX, 16, BLK), F32),
        pltpu.VMEM((NZ, 16, BLK), F32),
        pltpu.VMEM((NX, 8, BLK), F32),
        pltpu.VMEM((NCOL, NX, 8, BLK), F32),
        pltpu.SemaphoreType.DMA((NSEM,)),
        pltpu.SemaphoreType.DMA((NSEM,)),
    ]
    layer_out, feature_grad, weight_grad, bias_grad = pl.pallas_call(
        main_kernel,
        out_shape=(
            jax.ShapeDtypeStruct((2 * BLK, 2 * BLK), F32),
            jax.ShapeDtypeStruct((2 * BLK, BLK), F32),
            jax.ShapeDtypeStruct((BLK, 2 * BLK), F32),
            jax.ShapeDtypeStruct((1, 2 * BLK), F32),
        ),
        in_specs=[smem] + [vmem] * 6,
        out_specs=(vmem,) * 4,
        scratch_shapes=scratch,
        compiler_params=pltpu.CompilerParams(
            collective_id=0, has_side_effects=True, vmem_limit_bytes=58 * 2**20
        ),
    )(plan, features, node_ids, edge_blocks, weight, bias.reshape(1, -1), cotangent)
    return layer_out, feature_grad, weight_grad, bias_grad.reshape(-1)


def solution(mesh):
    return jax.shard_map(
        body,
        mesh=mesh,
        in_specs=(
            P(("col", "row"), None),
            P(("col", "row"), None),
            P(),
            P("row", "col", None),
            P("row", "col", None),
            P("row", "col", None),
            P("row", "col"),
            P(),
            P(),
            P(("row", "col"), None),
        ),
        out_specs=(P(("row", "col"), None), P(("col", "row"), None), P(), P()),
        check_vma=False,
    )
```

time: 696 us -> 96.7 us (0.14)
  waiting for transfers between devices: 361 us -> 0 us
  blocking collectives: 222 us -> 0 us
  Pallas kernels: 0 us -> 89.2 us
  matrix products: 44.2 us -> 0 us
  local copies, waits for them, and re-layouts: 46.9 us -> 6 us
  between operations: 14.5 us -> 1.29 us
    psum x1 -> x0, waiting for transfers between devices: 247 us -> none  [body(): lax.psum((weight_term * scale_factor, bias_term * scale_factor), ('row',...]
    psum x1 -> x0, blocking collectives: 222 us -> none  [body(): lax.psum((weight_term * scale_factor, bias_term * scale_factor), ('row',...]
    pallas_call x0 -> x2, Pallas kernels: none -> 89.2 us  [the longest x1 87.3 us: body(): pl.pallas_call(main_kernel, out_shape=(jax.ShapeDtypeStruct((2 * BLK, 2 *...]
    all_gather x2 -> x0, waiting for transfers between devices: 83.2 us -> none  [the longest x1 55 us: body(): column_strip = lax.all_gather(transformed, 'row', axis=0, tiled=True)]
    dot_general x11 -> x0, matrix products: 44.2 us -> none  [the longest x4 29.8 us: accumulate(): jnp.einsum('og,giw->oiw', selector, product, precision=highest)]
    reduce_scatter x2 -> x0, waiting for transfers between devices: 29.3 us -> none  [the longest x1 29.3 us: body(): lax.psum_scatter(partials, 'col', scatter_dimension=0, tiled=True) + bias]
    gather x9 -> x0, local copies, waits for them, and re-layouts: 24.6 us -> none  [the longest x2 12.3 us: accumulate(): picked = sources[cols_now]]
    while x6 -> x0, local copies, waits for them, and re-layouts: 14.1 us -> none  [the longest x2 14.1 us: block_sum(): totals = lax.fori_loop(0, turns, accumulate, start_totals)]
  transfers between devices with their start and end apart: 5 -> 0, of which waited for: 4 -> 0; matrix products, arithmetic and copies ran while one was open for 14% -> 0% of each run, Pallas kernels for 0% -> 0%
where the time goes in v1:
time: 96.7 us; the launch traced here: 96.5 us
  Pallas kernels  89.2 us (92%)
  local copies, waits for them, and re-layouts  6 us (6%)
  between operations  1.29 us (1%)
    pallas_call x1, Pallas kernels, body(): pl.pallas_call(main_kernel, out_shape=(jax.ShapeDtypeStruct((2 * BLK, 2 *...  87.3 us
    unnamed x4, local copies, waits for them, and re-layouts  6 us

profile of v1, /device:TPU:1, one launch (start us, length us, event | category | flops | bytes accessed | tf_op | source)
XLA Modules:
  0.0 96.5 jit_solution(15345410074475066304)
XLA Ops:
  1.3 1.9 %shard_map.129.idx = s32[8,384]{1,0:T(8,128)} custom-call(s32[1,1,256]{2,1,0:T(1,128)} %rows_ref.1, s32[1,1,256]{2,1,0:T(1,128)} %cols_ref.1, s32[1,1,256]{2,1,0:T(1,128)} %ids_ref.1, s32[1,1]{1,0:T(1,128)S(6)} %copy.18.live_ref), custom_call_target="tpu_custom_call" | custom-call | tf_op jit(solution)/shard_map/pallas_call | solution.py:531
  3.2 87.3 %shard_map.130 = (f32[256,256]{1,0:T(8,128)}, f32[256,128]{1,0:T(8,128)}, f32[128,256]{1,0:T(8,128)}, f32[1,256]{1,0:T(1,128)}) custom-call(s32[8,384]{1,0:T(8,128)} %shard_map.129.idx, bf16[256,128]{1,0:T(8,128)(2,1)} %feat.1, s32[1,256]{1,0:T(1,128)} %nid.1, bf16[64,128,128]{2,1,0:T(8,128)(2,1)} %edge.1, bf16[128,256]{1,0:T(8,128)(2,1)} %weight.1, ...), custom_call_target="tpu_custom_call" | custom-call | tf_op jit(solution)/shard_map/pallas_call | solution.py:565
  90.5 1.7 %copy.19 = f32[256,256]{1,0:T(8,128)} copy(f32[256,256]{1,0:T(8,128)} %get-tuple-element.16) | data formatting | bytes 524288
  92.2 1.6 %copy.20 = f32[256,128]{1,0:T(8,128)} copy(f32[256,128]{1,0:T(8,128)} %get-tuple-element.17) | data formatting | bytes 262144
  93.7 1.6 %copy.21 = f32[128,256]{1,0:T(8,128)} copy(f32[128,256]{1,0:T(8,128)} %get-tuple-element.18) | data formatting | bytes 262144
  95.3 1.2 %copy.22 = f32[256]{0:T(256)} copy(f32[256]{0:T(256)} %bitcast.3) | data formatting | bytes 2048

commit v2 on v1

v2 whole, which is shorter than its diff:
```python
import math

import jax
import jax.numpy as jnp
from jax import lax
from jax.experimental import pallas as pl
from jax.experimental.pallas import tpu as pltpu
from jax.sharding import PartitionSpec as P

F32 = jnp.float32
BF16 = jnp.bfloat16
I16 = jnp.int16
I32 = jnp.int32
MESH = pl.DeviceIdType.MESH

NX, NZ, NY, NCORE = 4, 8, 4, 2
NROW, NCOL = NX * NZ, NY * NCORE
NXY = NX * NY
BLK = 128
SLOTS = 256
FPAIRS = (SLOTS + 2 * NCOL) // 2
BPAIRS = (SLOTS + 2 * NROW) // 2
QLEN = 384
MSG = BLK + 16
SCALE = 1.0 / 256.0


def iota(shape, dim):
    return lax.broadcasted_iota(I32, shape, dim)


def to_column(row, size):
    eye = iota((size, size), 0) == iota((size, size), 1)
    return jnp.sum(jnp.where(eye, row, 0), axis=1, keepdims=True, dtype=I32)


def sort_direction(key, code, live, zero_source, empty_pair):
    key = jnp.where(iota((1, SLOTS), 1) < live, key, 1000)
    key_col = to_column(key, SLOTS)
    code_col = to_column(code, SLOTS)
    earlier = iota((SLOTS, SLOTS), 1) < iota((SLOTS, SLOTS), 0)
    same = jnp.where((key_col == key) & earlier, 1, 0)
    rank = jnp.sum(same, axis=1, keepdims=True, dtype=I32)
    names = iota((SLOTS, 128), 1)
    count = jnp.sum(jnp.where(key_col == names, 1, 0), axis=0, keepdims=True, dtype=I32)
    padded = (count + 1) & -2
    before = jnp.sum(jnp.where(names < key_col, padded, 0), axis=1, keepdims=True, dtype=I32)
    place = jnp.where(key_col < 999, before + rank, -1)
    spot = iota((SLOTS, QLEN), 1)
    picked = jnp.sum(jnp.where(place == spot, code_col, 0), axis=0, keepdims=True, dtype=I32)
    empty = picked == 0
    ids = jnp.where(empty, 0, lax.shift_right_logical(picked - 1, 7))
    src = jnp.where(empty, zero_source, (picked - 1) & 127)
    padded_col = to_column(padded, 128)
    count_col = to_column(count, 128)
    upper = iota((128, 128), 0) < iota((128, 128), 1)
    offset = jnp.sum(jnp.where(upper, padded_col, 0), axis=0, keepdims=True, dtype=I32)
    ends = jnp.where(count > 0, lax.shift_right_logical(offset + padded, 1) - 1, empty_pair)
    offset_col = to_column(offset, 128)
    start_col = jnp.where(count_col > 0, lax.shift_right_logical(offset_col, 1), -1)
    starts = jnp.where(start_col == iota((128, QLEN), 1), 1, 0)
    keep = 1 - jnp.sum(starts, axis=0, keepdims=True, dtype=I32)
    return ids, src, keep, ends


def plan_slots(rows_ref, cols_ref, ids_ref, live_ref, out_ref):
    live = live_ref[0, 0]
    rows = rows_ref[...].reshape(1, SLOTS)
    cols = cols_ref[...].reshape(1, SLOTS)
    ids = ids_ref[...].reshape(1, SLOTS)
    dev = lax.shift_right_logical(cols, 1)
    dev_x = lax.shift_right_logical(dev, 3)
    dev_z = dev & 7
    at_a = dev_z * NX + dev_x
    place = jnp.where((cols & 1) == 0, at_a, dev + NROW)
    f = sort_direction(rows, ids * 128 + place + 1, live, 2 * NROW, FPAIRS)
    b = sort_direction(place, ids * 128 + rows + 1, live, 2 * NCOL, BPAIRS)
    out_ref[...] = jnp.zeros((8, QLEN), I32)
    for k in range(3):
        out_ref[k : k + 1, :] = f[k]
        out_ref[3 + k : 4 + k, :] = b[k]
    out_ref[6:7, 0:128] = f[3]
    out_ref[7:8, 0:128] = b[3]


class Counter:
    def __init__(self):
        self.n = 0

    def take(self, *dims):
        base = self.n
        self.n += math.prod(dims)

        def at(*index):
            k = 0
            for d, i in zip(dims, index):
                assert 0 <= i < d
                k = k * d + i
            return base + k

        return at


def message_numbers():
    c = Counter()
    coded = dict(ra=(4, 4), la=(3, 4), xa=(3,), rb=(4,), lb=(3,), xb=(8, 3))
    plain = dict(
        ax=(4,), ar=(5, 4), al=(4, 4), br=(5,), bl=(4,), bx=(8, 4), cy=(4,), cs=(4,),
        ys=(4,), yy=(4,), g1=(1,), g2=(16,), g3=(8,), g4=(16,), g5=(1,),
    )
    table = {k: c.take(*d) for k, d in coded.items()}
    n_coded = c.n
    table.update({k: c.take(*d) for k, d in plain.items()})
    return table, n_coded, c.n


SEM, NCODED, NSEM = message_numbers()


def split(value):
    high = value.astype(BF16)
    low = (value - high.astype(F32)).astype(BF16)
    return high, low


def dot(a, b):
    return jnp.dot(a, b, preferred_element_type=F32)


def encode(value, ref):
    top = jnp.maximum(jnp.max(jnp.abs(value), axis=0, keepdims=True), 1e-30)
    e = jnp.ceil(jnp.log(top) * 256.0)
    q = jnp.round(value * (jnp.exp(e * (-1.0 / 256.0)) * 32000.0)).astype(I32)
    ref[0:BLK] = q.astype(I16)
    ref[BLK:MSG] = jnp.broadcast_to(e, (16, BLK)).astype(I32).astype(I16)


def decode(ref):
    e = ref[BLK:MSG].astype(I32).astype(F32)[0:1]
    return ref[0:BLK].astype(I32).astype(F32) * (jnp.exp(e * (1.0 / 256.0)) * (1.0 / 32000.0))


def main_kernel(
    live, rows, cols, ids, feat, nid, edge_hbm, weight, cot,
    agg_ref, gord_ref, grads_ref,
    plan_v, idx, edge, xs, cs, et, wt, sb, sf, ts, yb, sbuf, rbuf, ys_r, yy_r,
    wp, ws_r, p1_s, p1_r, p2_r, p3_r, ss, rs, ls,
):
    r = lax.axis_index("row")
    c = lax.axis_index("col")
    x, z = r // NZ, lax.rem(r, NZ)
    y, core = c // NCORE, lax.rem(c, NCORE)

    def xm(d):
        return lax.rem(x + d + NX, NX)

    def zm(d):
        return lax.rem(z + d + NZ, NZ)

    def ym(d):
        return lax.rem(y + d + NY, NY)

    def plane(px, pz):
        return (px * NZ + pz, c)

    def column(py, pc):
        return (r, py * NCORE + pc)

    def xy_peer(dx, dy):
        return (xm(dx) * NZ + z, ym(dy) * NCORE + core)

    started = []
    pending = {}

    def send(key, src, dst, dev):
        k = SEM[key[0]](*key[1:])
        d = pltpu.make_async_remote_copy(
            src_ref=src, dst_ref=dst, send_sem=ss.at[k], recv_sem=rs.at[k],
            device_id=dev, device_id_type=MESH,
        )
        d.start()
        pending[key] = d
        started.append(d)

    def recv(*key):
        pending.pop(key).wait_recv()

    xy_steps = [(a, b) for a in range(NX) for b in range(NY) if a or b]

    barrier = pltpu.get_barrier_semaphore()
    peers = [column(y, 1 - core)]
    peers += [plane(x, zm(d)) for d in (1, 7, 2, 6, 3, 5, 4)]
    peers += [xy_peer(*s) for s in xy_steps]
    for p in peers:
        pl.semaphore_signal(barrier, inc=1, device_id=p, device_id_type=MESH)
    edge_copy = pltpu.make_async_copy(edge_hbm, edge, ls.at[0])
    edge_copy.start()

    order = jnp.where(
        lax.broadcasted_iota(jnp.int32, (2 * BLK, 2 * BLK), 0) == nid[...], 1.0, 0.0
    )
    ordered = dot(order.T.astype(BF16), feat[...]).astype(BF16)
    xs[pl.ds(z * NX + x, 1)] = ordered[None, :BLK]
    xs[pl.ds(NROW + r, 1)] = ordered[None, BLK:]
    plan_slots(rows, cols, ids, live, plan_v)
    plan_copy = pltpu.make_async_copy(plan_v, idx, ls.at[1])
    plan_copy.start()
    wt[...] = weight[...].T
    pl.semaphore_wait(barrier, len(peers))

    def a_at(pz, px):
        return xs.at[pz * NX + px]

    def b_at(px, pz):
        return xs.at[NROW + px * NZ + pz]

    def ag_ar(s, f):
        o = a_at(zm(1 - s), xm(-f))
        send(("ar", s, f), o, o, plane(x, zm(1)))

    def ag_al(s, f):
        o = a_at(zm(s - 1), xm(-f))
        send(("al", s, f), o, o, plane(x, zm(-1)))

    def ag_br(s):
        o = b_at(x, zm(1 - s))
        send(("br", s), o, o, plane(x, zm(1)))

    def ag_bl(s):
        o = b_at(x, zm(s - 1))
        send(("bl", s), o, o, plane(x, zm(-1)))

    def ag_bx(rel):
        o = b_at(x, zm(-rel))
        for d in (2, 1, 3):
            send(("bx", rel, d), o, o, plane(xm(d), z))

    mine = cs.at[pl.ds(2 * c, 2)]
    for d in (2, 1, 3):
        send(("cy", d), cot, mine, column(ym(d), core))
    for d in (2, 1, 3):
        o = a_at(z, x)
        send(("ax", d), o, o, plane(xm(d), z))
    ag_ar(1, 0)
    ag_al(1, 0)
    ag_br(1)
    ag_bl(1)
    send(("cs", 0), cot, mine, column(y, 1 - core))
    ag_bx(0)
    cs[pl.ds(2 * c, 2)] = cot[...]

    xs[2 * NROW] = jnp.zeros((BLK, BLK), BF16)
    cs[2 * NCOL] = jnp.zeros((BLK, 2 * BLK), BF16)
    sb[BPAIRS] = jnp.zeros((BLK, 2 * BLK), F32)
    sf[FPAIRS] = jnp.zeros((BLK, BLK), F32)
    own_bias = jnp.sum(cot[...].reshape(2 * BLK, 2 * BLK).astype(F32), axis=0, keepdims=True) * SCALE
    bias_tile = jnp.concatenate(
        [own_bias[:, :BLK], own_bias[:, BLK:], jnp.zeros((6, BLK), F32)], axis=0
    )

    edge_copy.wait()
    plan_copy.wait()

    def turn(k, carry):
        for u in range(8):
            et[8 * k + u] = edge[8 * k + u].T
        return carry

    lax.fori_loop(0, 8, turn, 0)

    for f in (1, 3, 2):
        recv("ax", f)
        ag_ar(1, f)
        ag_al(1, f)
    for d in (1, 3, 2):
        recv("cy", d)
        o = cs.at[pl.ds(2 * (ym(-d) * NCORE + core), 2)]
        send(("cs", d), o, o, column(y, 1 - core))

    def ag_step(s):
        recv("br", s)
        if s < 4:
            ag_br(s + 1)
            recv("bl", s)
            if s < 3:
                ag_bl(s + 1)
        for f in (0, 1, 3, 2):
            recv("ar", s, f)
            if s < 4:
                ag_ar(s + 1, f)
                recv("al", s, f)
                if s < 3:
                    ag_al(s + 1, f)
        ag_bx(s)
        if s < 4:
            ag_bx(NZ - s)

    def run_pairs(lo, hi, unroll, total, body):
        assert (hi - lo) % unroll == 0

        def step(k, total):
            for u in range(unroll):
                total = body(lo + k * unroll + u, total)
            return total

        return lax.fori_loop(0, (hi - lo) // unroll, step, total)

    def back(p, total):
        e0, e1 = idx[3, 2 * p], idx[3, 2 * p + 1]
        left = jnp.concatenate([et[e0], et[e1]], axis=1)
        right = jnp.concatenate([cs[idx[4, 2 * p]], cs[idx[4, 2 * p + 1]]], axis=0)
        total = total * idx[5, p].astype(F32) + dot(left, right)
        sb[pl.ds(p, 1)] = total[None]
        return total

    def forth(p, total):
        e0, e1 = idx[0, 2 * p], idx[0, 2 * p + 1]
        left = jnp.concatenate([edge[e0], edge[e1]], axis=1)
        right = jnp.concatenate([xs[idx[1, 2 * p]], xs[idx[1, 2 * p + 1]]], axis=0)
        total = total * idx[2, p].astype(F32) + dot(left, right)
        sf[pl.ds(p, 1)] = total[None]
        return total

    ag_step(1)
    for d in range(NY):
        recv("cs", d)
    total = run_pairs(0, 80, 16, jnp.zeros((BLK, 2 * BLK), F32), back)
    ag_step(2)
    run_pairs(80, 160, 16, total, back)
    ag_step(3)

    def stage(k, carry):
        for u in range(8):
            at = 8 * k + u
            high, low = split(sb[idx[7, at]])
            ts[pl.ds(at, 1)] = (dot(high, wt[...]) + dot(low, wt[...]))[None]
        return carry

    lax.fori_loop(0, 2 * NROW // 8, stage, 0)

    def t_a(pz, px):
        return pz * NX + px

    def t_b(px, pz):
        return NROW + px * NZ + pz

    def post(key, value, dev):
        k = SEM[key[0]](*key[1:])
        encode(value, sbuf.at[k])
        send(key, sbuf.at[k], rbuf.at[k], dev)

    def take(*key):
        recv(*key)
        return decode(rbuf.at[SEM[key[0]](*key[1:])])

    def rs_ra(s, f):
        v = ts[t_a(zm(4 - s), xm(f))]
        if s:
            v = v + take("ra", s - 1, f)
        post(("ra", s, f), v, plane(x, zm(1)))

    def rs_la(s, f):
        v = ts[t_a(zm(s - 3), xm(f))]
        if s:
            v = v + take("la", s - 1, f)
        post(("la", s, f), v, plane(x, zm(-1)))

    def rs_bx(rel):
        for d in (2, 1, 3):
            post(("xb", rel, d - 1), ts[t_b(xm(d), zm(rel))], plane(xm(d), z))

    def rs_bg(rel):
        v = ts[t_b(x, zm(rel))]
        for d in range(1, NX):
            v = v + take("xb", rel, d - 1)
        return v

    def rs_rb(s):
        v = rs_bg((4 - s) % NZ)
        if s:
            v = v + take("rb", s - 1)
        post(("rb", s), v, plane(x, zm(1)))

    def rs_lb(s):
        v = rs_bg((s - 3) % NZ)
        if s:
            v = v + take("lb", s - 1)
        post(("lb", s), v, plane(x, zm(-1)))

    def rs_a(s):
        for f in range(NX):
            rs_ra(s, f)
            if s < 3:
                rs_la(s, f)

    rs_a(0)
    rs_bx(4)
    rs_bx(5)
    ag_step(4)
    for rel in (3, 6, 2, 7, 1, 0):
        rs_bx(rel)

    def grad(k, acc):
        for u in range(8):
            at = 8 * k + u
            xt = xs[at].T
            high, low = split(sb[idx[7, at]])
            acc = acc + dot(
                jnp.concatenate([xt, xt], axis=1), jnp.concatenate([high, low], axis=0)
            )
        return acc

    acc = lax.fori_loop(0, NROW // 8, grad, jnp.zeros((BLK, 2 * BLK), F32))
    for rel in range(NZ):
        for d in range(1, NX):
            recv("bx", rel, d)
    acc = lax.fori_loop(NROW // 8, 2 * NROW // 8, grad, acc) * SCALE
    for t in range(2 * NXY):
        a, b = 8 * (t // 2), BLK * (t % 2)
        wp[t // NXY, t % NXY] = acc[a : a + 8, b : b + BLK]
    send(("g1", 0), wp.at[1 - core], ws_r, column(y, 1 - core))

    rs_a(1)
    rs_rb(0)
    rs_lb(0)

    recv("g1", 0)
    me = x * NY + y
    p1_s[:, 0:8] = wp[core] + ws_r[...]
    for t in range(NXY):
        p1_s[t, 8:16] = bias_tile
    p1_r[pl.ds(me, 1)] = p1_s[pl.ds(me, 1)]
    for i, (a, b) in enumerate(xy_steps):
        send(("g2", i), p1_s.at[xm(a) * NY + ym(b)], p1_r.at[me], xy_peer(a, b))

    total = run_pairs(0, 68, 17, jnp.zeros((BLK, BLK), F32), forth)
    rs_a(2)
    rs_rb(1)
    rs_lb(1)
    for i in range(len(xy_steps)):
        recv("g2", i)
    tile = p1_r[0]
    for k in range(1, NXY):
        tile = tile + p1_r[k]
    p2_r[pl.ds(z, 1)] = tile[None]
    for d in (4, 3, 5, 2, 6, 1, 7):
        send(("g3", d), p2_r.at[z], p2_r.at[z], plane(x, zm(d)))

    run_pairs(68, 136, 17, total, forth)

    def stage_y(k, carry):
        for u in range(4):
            yb[4 * k + u] = sf[idx[6, 4 * k + u]]
        return carry

    lax.fori_loop(0, 2 * NCOL // 4, stage_y, 0)
    for py in range(NY):
        at = 2 * (py * NCORE + 1 - core)
        send(("ys", py), yb.at[pl.ds(at, 2)], ys_r.at[py], column(y, 1 - core))

    for d in range(1, NZ):
        recv("g3", d)
    tile = p2_r[0]
    for k in range(1, NZ):
        tile = tile + p2_r[k]
    p3_r[pl.ds(core, 1), pl.ds(me, 1)] = tile[None, None, 0:8]
    p3_r[pl.ds(core, 1), NXY : NXY + 1] = tile[None, None, 8:16]
    for i, (a, b) in enumerate(xy_steps):
        o = p3_r.at[core, me]
        send(("g4", i), o, o, xy_peer(a, b))

    for py in range(NY):
        recv("ys", py)
    for py in range(NY):
        at = 2 * (py * NCORE + core)
        yb[pl.ds(at, 2)] = yb[pl.ds(at, 2)] + ys_r[py]
    for d in (2, 1, 3):
        at = 2 * (ym(d) * NCORE + core)
        send(("yy", d), yb.at[pl.ds(at, 2)], yy_r.at[d - 1], column(ym(d), core))

    rs_a(3)
    rs_rb(2)
    rs_lb(2)

    own_a = None
    for f in (1, 2, 3, 0):
        v = ts[t_a(z, xm(f))] + take("ra", 3, f) + take("la", 2, f)
        if f:
            post(("xa", f - 1), v, plane(xm(f), z))
        else:
            own_a = v
    rs_rb(3)
    own_b = rs_bg(0) + take("lb", 2)

    for i in range(len(xy_steps)):
        recv("g4", i)
    o = p3_r.at[core]
    send(("g5", 0), o, o, column(y, 1 - core))

    for d in range(1, NY):
        recv("yy", d)
    agg = yb[pl.ds(2 * c, 2)]
    for d in range(1, NY):
        agg = agg + yy_r[d - 1]
    agg_ref[...] = agg.reshape(2 * BLK, BLK)

    own_b = own_b + take("rb", 3)
    for f in range(1, NX):
        own_a = own_a + take("xa", f - 1)
    gord_ref[0:BLK] = own_a
    gord_ref[BLK : 2 * BLK] = own_b
    recv("g5", 0)
    grads_ref[...] = p3_r[...]

    assert not pending, pending.keys()
    for d in started:
        d.wait_send()


def final_kernel(agg, gord, grads, nid, weight, bias, out_ref, fg_ref, wg_ref, bg_ref):
    high, low = split(agg[...])
    out_ref[...] = dot(high, weight[...]) + dot(low, weight[...]) + bias[...]
    order = jnp.where(
        lax.broadcasted_iota(jnp.int32, (2 * BLK, 2 * BLK), 0) == nid[...], 1.0, 0.0
    ).astype(BF16)
    high, low = split(gord[...])
    fg_ref[...] = dot(order, high) + dot(order, low)
    for t in range(2 * NXY):
        a, b = 8 * (t // 2), BLK * (t % 2)
        wg_ref[a : a + 8, b : b + BLK] = grads[t // NXY, t % NXY]
    tile = grads[0, NXY] + grads[1, NXY]
    bg_ref[...] = jnp.concatenate([tile[0:1], tile[1:2]], axis=1)


def body(
    features, node_ids, edge_blocks, block_rows, block_cols, block_ids, live_blocks,
    weight, bias, cotangent,
):
    vmem = pl.BlockSpec(memory_space=pltpu.VMEM)
    smem = pl.BlockSpec(memory_space=pltpu.SMEM)
    tile = (BLK, BLK)
    scratch = [
        pltpu.VMEM((8, QLEN), I32),
        pltpu.SMEM((8, QLEN), I32),
        pltpu.VMEM((64, *tile), BF16),
        pltpu.VMEM((2 * NROW + 1, *tile), BF16),
        pltpu.VMEM((2 * NCOL + 1, BLK, 2 * BLK), BF16),
        pltpu.VMEM((64, *tile), BF16),
        pltpu.VMEM((2 * BLK, BLK), BF16),
        pltpu.VMEM((BPAIRS + 1, BLK, 2 * BLK), F32),
        pltpu.VMEM((FPAIRS + 1, *tile), F32),
        pltpu.VMEM((2 * NROW, *tile), F32),
        pltpu.VMEM((2 * NCOL, *tile), F32),
        pltpu.VMEM((NCODED, MSG, BLK), I16),
        pltpu.VMEM((NCODED, MSG, BLK), I16),
        pltpu.VMEM((NY, 2, *tile), F32),
        pltpu.VMEM((NY - 1, 2, *tile), F32),
        pltpu.VMEM((2, NXY, 8, BLK), F32),
        pltpu.VMEM((NXY, 8, BLK), F32),
        pltpu.VMEM((NXY, 16, BLK), F32),
        pltpu.VMEM((NXY, 16, BLK), F32),
        pltpu.VMEM((NZ, 16, BLK), F32),
        pltpu.VMEM((2, NXY + 1, 8, BLK), F32),
        pltpu.SemaphoreType.DMA((NSEM,)),
        pltpu.SemaphoreType.DMA((NSEM,)),
        pltpu.SemaphoreType.DMA((2,)),
    ]
    agg, gord, grads = pl.pallas_call(
        main_kernel,
        out_shape=(
            jax.ShapeDtypeStruct((2 * BLK, BLK), F32),
            jax.ShapeDtypeStruct((2 * BLK, BLK), F32),
            jax.ShapeDtypeStruct((2, NXY + 1, 8, BLK), F32),
        ),
        in_specs=[smem] + [vmem] * 5 + [pl.BlockSpec(memory_space=pl.ANY)] + [vmem] * 2,
        out_specs=(vmem,) * 3,
        scratch_shapes=scratch,
        compiler_params=pltpu.CompilerParams(
            collective_id=0, has_side_effects=True, vmem_limit_bytes=58 * 2**20
        ),
    )(
        live_blocks, block_rows, block_cols, block_ids, features, node_ids, edge_blocks,
        weight, cotangent.reshape(2, BLK, 2 * BLK),
    )
    layer_out, feature_grad, weight_grad, bias_grad = pl.pallas_call(
        final_kernel,
        out_shape=(
            jax.ShapeDtypeStruct((2 * BLK, 2 * BLK), F32),
            jax.ShapeDtypeStruct((2 * BLK, BLK), F32),
            jax.ShapeDtypeStruct((BLK, 2 * BLK), F32),
            jax.ShapeDtypeStruct((1, 2 * BLK), F32),
        ),
        in_specs=[vmem] * 6,
        out_specs=(vmem,) * 4,
    )(agg, gord, grads, node_ids, weight, bias.reshape(1, -1))
    return layer_out, feature_grad, weight_grad, bias_grad.reshape(-1)


def solution(mesh):
    return jax.shard_map(
        body,
        mesh=mesh,
        in_specs=(
            P(("col", "row"), None),
            P(("col", "row"), None),
            P(),
            P("row", "col", None),
            P("row", "col", None),
            P("row", "col", None),
            P("row", "col"),
            P(),
            P(),
            P(("row", "col"), None),
        ),
        out_specs=(P(("row", "col"), None), P(("col", "row"), None), P(), P()),
        check_vma=False,
    )
```

time: 96.7 us -> 72.8 us (0.75)
  Pallas kernels: 89.2 us -> 71.4 us
  local copies, waits for them, and re-layouts: 6 us -> 0 us
    pallas_call x2, Pallas kernels: 89.2 us -> 71.4 us  [the longest x1 69.3 us: body(): pl.pallas_call(main_kernel, out_shape=(jax.ShapeDtypeStruct((2 * BLK, BLK...]
    unnamed x4 -> x0, local copies, waits for them, and re-layouts: 6 us -> none
where the time goes in v2:
time: 72.8 us; the launch traced here: 72.7 us
  Pallas kernels  71.4 us (98%)
  between operations  1.29 us (2%)
    pallas_call x1, Pallas kernels, body(): pl.pallas_call(main_kernel, out_shape=(jax.ShapeDtypeStruct((2 * BLK, BLK...  69.3 us
    pallas_call x1, Pallas kernels, body(): pl.pallas_call(final_kernel, out_shape=(jax.ShapeDtypeStruct((2 * BLK, 2...  2.14 us

profile of v2, /device:TPU:1, one launch (start us, length us, event | category | flops | bytes accessed | tf_op | source)
XLA Modules:
  0.0 72.7 jit_solution(9190528618531526692)
XLA Ops:
  1.3 69.3 %shard_map.129 = (f32[256,128]{1,0:T(8,128)}, f32[256,128]{1,0:T(8,128)}, f32[2,17,8,128]{3,2,1,0:T(8,128)}) custom-call(s32[1,1]{1,0:T(1,128)S(6)} %copy.14.live, s32[1,1,256]{2,1,0:T(1,128)} %rows.1, s32[1,1,256]{2,1,0:T(1,128)} %cols.1, s32[1,1,256]{2,1,0:T(1,128)} %ids.1, bf16[256,128]{1,0:T(8,128)(2,1)} %feat.1, s32[1,256]{1,0:T(1,128)} %nid.3, ...), custom_call_target="tpu_custom_call" | custom-call | tf_op jit(solution)/shard_map/pallas_call | solution.py:568
  70.6 2.1 %shard_map.130 = (f32[256,256]{1,0:T(8,128)}, f32[256,128]{1,0:T(8,128)}, f32[128,256]{1,0:T(8,128)}, f32[1,256]{1,0:T(1,128)}) custom-call(f32[256,128]{1,0:T(8,128)} %get-tuple-element.11.agg, f32[256,128]{1,0:T(8,128)} %get-tuple-element.12.gord, f32[2,17,8,128]{3,2,1,0:T(8,128)} %get-tuple-element.13.grads, s32[1,256]{1,0:T(1,128)} %nid.3, ...), custom_call_target="tpu_custom_call" | custom-call | tf_op jit(solution)/shard_map/pallas_call | solution.py:585

commit v3 on v2

--- a/solution.py
+++ b/solution.py
@@ -64,7 +64,7 @@
 
 
 def plan_slots(rows_ref, cols_ref, ids_ref, live_ref, out_ref):
-    live = live_ref[0, 0]
+    live = live_ref[...]
     rows = rows_ref[...].reshape(1, SLOTS)
     cols = cols_ref[...].reshape(1, SLOTS)
     ids = ids_ref[...].reshape(1, SLOTS)
@@ -103,10 +103,10 @@
 
 def message_numbers():
     c = Counter()
-    coded = dict(ra=(4, 4), la=(3, 4), xa=(3,), rb=(4,), lb=(3,), xb=(8, 3))
+    coded = dict(ra=(4, 4), la=(3, 4), xa=(3,), rb=(4,), lb=(3,), xb=(3, 8))
     plain = dict(
-        ax=(4,), ar=(5, 4), al=(4, 4), br=(5,), bl=(4,), bx=(8, 4), cy=(4,), cs=(4,),
-        ys=(4,), yy=(4,), g1=(1,), g2=(16,), g3=(8,), g4=(16,), g5=(1,),
+        ax=(4,), ar=(5, 4), al=(4, 4), br=(5,), bl=(4,), bx=(8, 4), cy=(4, 2), cs=(4, 2),
+        ys=(4,), yy=(4,), g1=(1,), g2=(8,), g3=(16,), g4=(8,), g5=(1,),
     )
     table = {k: c.take(*d) for k, d in coded.items()}
     n_coded = c.n
@@ -141,9 +141,10 @@
 
 
 def main_kernel(
-    live, rows, cols, ids, feat, nid, edge_hbm, weight, cot,
+    live_h, rows_h, cols_h, ids_h, feat_h, nid_h, edge_h, weight_h, cot_h,
     agg_ref, gord_ref, grads_ref,
-    plan_v, idx, edge, xs, cs, et, wt, sb, sf, ts, yb, sbuf, rbuf, ys_r, yy_r,
+    live, rows, cols, ids, feat, nid, edge, weight,
+    plan_v, idx, xs, cs, phl, et, sb, sf, ts, yb, sbuf, rbuf, ys_r, yy_r,
     wp, ws_r, p1_s, p1_r, p2_r, p3_r, ss, rs, ls,
 ):
     r = lax.axis_index("row")
@@ -188,24 +189,34 @@
     xy_steps = [(a, b) for a in range(NX) for b in range(NY) if a or b]
 
     barrier = pltpu.get_barrier_semaphore()
-    peers = [column(y, 1 - core)]
-    peers += [plane(x, zm(d)) for d in (1, 7, 2, 6, 3, 5, 4)]
-    peers += [xy_peer(*s) for s in xy_steps]
+    peers = [plane(x, zm(1)), plane(x, zm(-1))]
+    peers += [plane(xm(d), z) for d in range(1, NX)]
+    peers += [column(ym(d), core) for d in range(1, NY)]
+    peers += [column(y, 1 - core)]
     for p in peers:
         pl.semaphore_signal(barrier, inc=1, device_id=p, device_id_type=MESH)
-    edge_copy = pltpu.make_async_copy(edge_hbm, edge, ls.at[0])
-    edge_copy.start()
-
-    order = jnp.where(
-        lax.broadcasted_iota(jnp.int32, (2 * BLK, 2 * BLK), 0) == nid[...], 1.0, 0.0
-    )
-    ordered = dot(order.T.astype(BF16), feat[...]).astype(BF16)
-    xs[pl.ds(z * NX + x, 1)] = ordered[None, :BLK]
-    xs[pl.ds(NROW + r, 1)] = ordered[None, BLK:]
+    loads = {}
+    for k, (name, src, dst) in enumerate([
+        ("feat", feat_h, feat), ("nid", nid_h, nid),
+        ("cot", cot_h, cs.at[pl.ds(2 * c, 2)]), ("rows", rows_h, rows), ("cols", cols_h, cols),
+        ("ids", ids_h, ids), ("live", live_h, live), ("weight", weight_h, weight),
+        ("edge", edge_h, edge),
+    ]):
+        loads[name] = pltpu.make_async_copy(src, dst, ls.at[k])
+        loads[name].start()
+
+    loads["feat"].wait()
+    loads["nid"].wait()
+    order = jnp.where(iota((2 * BLK, 2 * BLK), 0) == nid[...], 1.0, 0.0)
+    ordered = dot(feat[...].T, order.astype(BF16)).astype(BF16)
+    xs[pl.ds(z * NX + x, 1)] = ordered[None, :, :BLK]
+    xs[pl.ds(NROW + r, 1)] = ordered[None, :, BLK:]
+    for name in ("rows", "cols", "ids", "live"):
+        loads[name].wait()
     plan_slots(rows, cols, ids, live, plan_v)
-    plan_copy = pltpu.make_async_copy(plan_v, idx, ls.at[1])
+    plan_copy = pltpu.make_async_copy(plan_v, idx, ls.at[len(loads)])
     plan_copy.start()
-    wt[...] = weight[...].T
+    loads["cot"].wait()
     pl.semaphore_wait(barrier, len(peers))
 
     def a_at(pz, px):
@@ -235,65 +246,90 @@
         for d in (2, 1, 3):
             send(("bx", rel, d), o, o, plane(xm(d), z))
 
-    mine = cs.at[pl.ds(2 * c, 2)]
+    own = a_at(z, x)
+    ag_br(1)
+    ag_bl(1)
     for d in (2, 1, 3):
-        send(("cy", d), cot, mine, column(ym(d), core))
-    for d in (2, 1, 3):
-        o = a_at(z, x)
-        send(("ax", d), o, o, plane(xm(d), z))
+        send(("ax", d), own, own, plane(xm(d), z))
     ag_ar(1, 0)
     ag_al(1, 0)
-    ag_br(1)
-    ag_bl(1)
-    send(("cs", 0), cot, mine, column(y, 1 - core))
+    for h in range(2):
+        o = cs.at[2 * c + h]
+        for d in (2, 1, 3):
+            send(("cy", d, h), o, o, column(ym(d), core))
+    for h in range(2):
+        o = cs.at[2 * c + h]
+        send(("cs", 0, h), o, o, column(y, 1 - core))
     ag_bx(0)
-    cs[pl.ds(2 * c, 2)] = cot[...]
 
     xs[2 * NROW] = jnp.zeros((BLK, BLK), BF16)
-    cs[2 * NCOL] = jnp.zeros((BLK, 2 * BLK), BF16)
-    sb[BPAIRS] = jnp.zeros((BLK, 2 * BLK), F32)
+    phl[2 * NCOL] = jnp.zeros((BLK, 2 * BLK), BF16)
+    sb[BPAIRS] = jnp.zeros((BLK, BLK), F32)
     sf[FPAIRS] = jnp.zeros((BLK, BLK), F32)
-    own_bias = jnp.sum(cot[...].reshape(2 * BLK, 2 * BLK).astype(F32), axis=0, keepdims=True) * SCALE
-    bias_tile = jnp.concatenate(
-        [own_bias[:, :BLK], own_bias[:, BLK:], jnp.zeros((6, BLK), F32)], axis=0
-    )
-
-    edge_copy.wait()
-    plan_copy.wait()
-
-    def turn(k, carry):
-        for u in range(8):
-            et[8 * k + u] = edge[8 * k + u].T
-        return carry
-
-    lax.fori_loop(0, 8, turn, 0)
-
-    for f in (1, 3, 2):
-        recv("ax", f)
-        ag_ar(1, f)
-        ag_al(1, f)
-    for d in (1, 3, 2):
-        recv("cy", d)
-        o = cs.at[pl.ds(2 * (ym(-d) * NCORE + core), 2)]
-        send(("cs", d), o, o, column(y, 1 - core))
-
-    def ag_step(s):
+
+    def ag_b(s):
         recv("br", s)
         if s < 4:
             ag_br(s + 1)
             recv("bl", s)
             if s < 3:
                 ag_bl(s + 1)
-        for f in (0, 1, 3, 2):
+        ag_bx(s)
+        if s < 4:
+            ag_bx(NZ - s)
+
+    def ag_a(s, flows=(0, 1, 3, 2)):
+        for f in flows:
             recv("ar", s, f)
             if s < 4:
                 ag_ar(s + 1, f)
                 recv("al", s, f)
                 if s < 3:
                     ag_al(s + 1, f)
-        ag_bx(s)
-        if s < 4:
-            ag_bx(NZ - s)
+
+    ag_b(1)
+    for f in (1, 3, 2):
+        recv("ax", f)
+        ag_ar(1, f)
+        ag_al(1, f)
+    ag_a(1, (0,))
+    ag_b(2)
+    ag_a(1, (1, 3, 2))
+    ag_a(2, (0,))
+    loads["weight"].wait()
+    loads["edge"].wait()
+
+    def turn(k, carry):
+        for u in range(8):
+            et[8 * k + u] = edge[8 * k + u].T
+        return carry
+
+    lax.fori_loop(0, 8, turn, 0)
+
+    for h in range(2):
+        for d in (1, 3, 2):
+            recv("cy", d, h)
+            o = cs.at[2 * (ym(-d) * NCORE + core) + h]
+            send(("cs", d, h), o, o, column(y, 1 - core))
+
+    wt = weight[...].T
+
+    def project(k):
+        strip = cs[pl.ds(2 * k, 2)].reshape(2 * BLK, 2 * BLK)
+        high, low = split(dot(strip, wt))
+        both = jnp.concatenate([high, low], axis=1)
+        phl[pl.ds(2 * k, 2)] = both.reshape(2, BLK, 2 * BLK)
+
+    for d in range(NY):
+        project(ym(d) * NCORE + core)
+    ag_b(3)
+    ag_a(2, (1, 3, 2))
+    for h in range(2):
+        for d in range(NY):
+            recv("cs", d, h)
+    for d in range(NY):
+        project(ym(d) * NCORE + 1 - core)
+    plan_copy.wait()
 
     def run_pairs(lo, hi, unroll, total, body):
         assert (hi - lo) % unroll == 0
@@ -305,35 +341,37 @@
 
         return lax.fori_loop(0, (hi - lo) // unroll, step, total)
 
-    def back(p, total):
-        e0, e1 = idx[3, 2 * p], idx[3, 2 * p + 1]
-        left = jnp.concatenate([et[e0], et[e1]], axis=1)
-        right = jnp.concatenate([cs[idx[4, 2 * p]], cs[idx[4, 2 * p + 1]]], axis=0)
-        total = total * idx[5, p].astype(F32) + dot(left, right)
-        sb[pl.ds(p, 1)] = total[None]
-        return total
-
-    def forth(p, total):
-        e0, e1 = idx[0, 2 * p], idx[0, 2 * p + 1]
-        left = jnp.concatenate([edge[e0], edge[e1]], axis=1)
-        right = jnp.concatenate([xs[idx[1, 2 * p]], xs[idx[1, 2 * p + 1]]], axis=0)
-        total = total * idx[2, p].astype(F32) + dot(left, right)
-        sf[pl.ds(p, 1)] = total[None]
-        return total
-
-    ag_step(1)
-    for d in range(NY):
-        recv("cs", d)
-    total = run_pairs(0, 80, 16, jnp.zeros((BLK, 2 * BLK), F32), back)
-    ag_step(2)
-    run_pairs(80, 160, 16, total, back)
-    ag_step(3)
+    def pair(base, forward, sums):
+        def run(p, total):
+            e0, e1 = idx[base, 2 * p], idx[base, 2 * p + 1]
+            s0, s1 = idx[base + 1, 2 * p], idx[base + 1, 2 * p + 1]
+            if forward:
+                left = jnp.concatenate([xs[s0], xs[s1]], axis=1)
+                right = jnp.concatenate([et[e0], et[e1]], axis=0)
+            else:
+                left = jnp.concatenate([et[e0], et[e1]], axis=1)
+                right = jnp.concatenate([phl[s0], phl[s1]], axis=0)
+            prod = dot(left, right)
+            if prod.shape[1] == 2 * BLK:
+                prod = prod[:, :BLK] + prod[:, BLK:]
+            total = total * idx[base + 2, p].astype(F32) + prod
+            sums[pl.ds(p, 1)] = total[None]
+            return total
+
+        return run
+
+    back = pair(3, False, sb)
+    forth = pair(0, True, sf)
+
+    zero = jnp.zeros((BLK, BLK), F32)
+    total = run_pairs(0, 80, 20, zero, back)
+    ag_b(4)
+    ag_a(3)
+    run_pairs(80, 160, 20, total, back)
 
     def stage(k, carry):
         for u in range(8):
-            at = 8 * k + u
-            high, low = split(sb[idx[7, at]])
-            ts[pl.ds(at, 1)] = (dot(high, wt[...]) + dot(low, wt[...]))[None]
+            ts[8 * k + u] = sb[idx[7, 8 * k + u]]
         return carry
 
     lax.fori_loop(0, 2 * NROW // 8, stage, 0)
@@ -343,6 +381,40 @@
 
     def t_b(px, pz):
         return NROW + px * NZ + pz
+
+    def b_value(px, pz):
+        return ts[t_b(px, pz)]
+
+    def send_many(key, k, src, dst, dev):
+        d = pltpu.make_async_remote_copy(
+            src_ref=src, dst_ref=dst, send_sem=ss.at[k], recv_sem=rs.at[k],
+            device_id=dev, device_id_type=MESH,
+        )
+        d.start()
+        pending[key] = d
+        started.append(d)
+
+    b_order = (4, 5, 3, 6, 2, 7, 1, 0)
+    b_groups = ((0, 2), (2, 4), (4, 6), (6, 8))
+
+    def rs_bx(g):
+        lo, hi = b_groups[g]
+        for d in (2, 1, 3):
+            base = SEM["xb"](d - 1, lo)
+            for i in range(lo, hi):
+                encode(b_value(xm(d), zm(b_order[i])), sbuf.at[base + i - lo])
+            part = pl.ds(base, hi - lo)
+            send_many(("xb", d, g), base, sbuf.at[part], rbuf.at[part], plane(xm(d), z))
+
+    def rs_bx_recv(g):
+        for d in range(1, NX):
+            recv("xb", d, g)
+
+    def rs_bg(rel):
+        v = b_value(x, zm(rel))
+        for d in range(1, NX):
+            v = v + decode(rbuf.at[SEM["xb"](d - 1, b_order.index(rel))])
+        return v
 
     def post(key, value, dev):
         k = SEM[key[0]](*key[1:])
@@ -353,27 +425,17 @@
         recv(*key)
         return decode(rbuf.at[SEM[key[0]](*key[1:])])
 
-    def rs_ra(s, f):
-        v = ts[t_a(zm(4 - s), xm(f))]
-        if s:
-            v = v + take("ra", s - 1, f)
-        post(("ra", s, f), v, plane(x, zm(1)))
-
-    def rs_la(s, f):
-        v = ts[t_a(zm(s - 3), xm(f))]
-        if s:
-            v = v + take("la", s - 1, f)
-        post(("la", s, f), v, plane(x, zm(-1)))
-
-    def rs_bx(rel):
-        for d in (2, 1, 3):
-            post(("xb", rel, d - 1), ts[t_b(xm(d), zm(rel))], plane(xm(d), z))
-
-    def rs_bg(rel):
-        v = ts[t_b(x, zm(rel))]
-        for d in range(1, NX):
-            v = v + take("xb", rel, d - 1)
-        return v
+    def rs_a(s):
+        for f in range(NX):
+            v = ts[t_a(zm(4 - s), xm(f))]
+            if s:
+                v = v + take("ra", s - 1, f)
+            post(("ra", s, f), v, plane(x, zm(1)))
+            if s < 3:
+                v = ts[t_a(zm(s - 3), xm(f))]
+                if s:
+                    v = v + take("la", s - 1, f)
+                post(("la", s, f), v, plane(x, zm(-1)))
 
     def rs_rb(s):
         v = rs_bg((4 - s) % NZ)
@@ -387,88 +449,66 @@
             v = v + take("lb", s - 1)
         post(("lb", s), v, plane(x, zm(-1)))
 
-    def rs_a(s):
-        for f in range(NX):
-            rs_ra(s, f)
-            if s < 3:
-                rs_la(s, f)
-
+    def rs_b(s):
+        rs_bx_recv(s)
+        rs_rb(s)
+        if s < 3:
+            rs_lb(s)
+
+    rs_bx(0)
     rs_a(0)
-    rs_bx(4)
-    rs_bx(5)
-    ag_step(4)
-    for rel in (3, 6, 2, 7, 1, 0):
-        rs_bx(rel)
-
-    def grad(k, acc):
-        for u in range(8):
-            at = 8 * k + u
-            xt = xs[at].T
-            high, low = split(sb[idx[7, at]])
-            acc = acc + dot(
-                jnp.concatenate([xt, xt], axis=1), jnp.concatenate([high, low], axis=0)
-            )
-        return acc
-
-    acc = lax.fori_loop(0, NROW // 8, grad, jnp.zeros((BLK, 2 * BLK), F32))
-    for rel in range(NZ):
+    for g in (1, 2, 3):
+        rs_bx(g)
+
+    ag_a(4)
+    for rel in (0, 1, 7, 2, 6, 3, 5, 4):
         for d in range(1, NX):
             recv("bx", rel, d)
-    acc = lax.fori_loop(NROW // 8, 2 * NROW // 8, grad, acc) * SCALE
+
+    run_pairs(0, 136, 17, zero, forth)
+
+    def stage_y(k, carry):
+        for u in range(4):
+            yb[4 * k + u] = sf[idx[6, 4 * k + u]]
+        return carry
+
+    lax.fori_loop(0, 2 * NCOL // 4, stage_y, 0)
+    def grad(k, acc):
+        for u in range(2):
+            at = 4 * k + 2 * u
+            strip = cs[pl.ds(at, 2)].reshape(2 * BLK, 2 * BLK)
+            high, low = split(jnp.concatenate([yb[at], yb[at + 1]], axis=1))
+            acc = acc + dot(high, strip) + dot(low, strip)
+        return acc
+
+    acc = lax.fori_loop(0, NCOL // 2, grad, jnp.zeros((BLK, 2 * BLK), F32)) * SCALE
     for t in range(2 * NXY):
         a, b = 8 * (t // 2), BLK * (t % 2)
         wp[t // NXY, t % NXY] = acc[a : a + 8, b : b + BLK]
     send(("g1", 0), wp.at[1 - core], ws_r, column(y, 1 - core))
 
-    rs_a(1)
-    rs_rb(0)
-    rs_lb(0)
-
-    recv("g1", 0)
-    me = x * NY + y
-    p1_s[:, 0:8] = wp[core] + ws_r[...]
-    for t in range(NXY):
-        p1_s[t, 8:16] = bias_tile
-    p1_r[pl.ds(me, 1)] = p1_s[pl.ds(me, 1)]
-    for i, (a, b) in enumerate(xy_steps):
-        send(("g2", i), p1_s.at[xm(a) * NY + ym(b)], p1_r.at[me], xy_peer(a, b))
-
-    total = run_pairs(0, 68, 17, jnp.zeros((BLK, BLK), F32), forth)
-    rs_a(2)
-    rs_rb(1)
-    rs_lb(1)
-    for i in range(len(xy_steps)):
-        recv("g2", i)
-    tile = p1_r[0]
-    for k in range(1, NXY):
-        tile = tile + p1_r[k]
-    p2_r[pl.ds(z, 1)] = tile[None]
-    for d in (4, 3, 5, 2, 6, 1, 7):
-        send(("g3", d), p2_r.at[z], p2_r.at[z], plane(x, zm(d)))
-
-    run_pairs(68, 136, 17, total, forth)
-
-    def stage_y(k, carry):
-        for u in range(4):
-            yb[4 * k + u] = sf[idx[6, 4 * k + u]]
-        return carry
-
-    lax.fori_loop(0, 2 * NCOL // 4, stage_y, 0)
     for py in range(NY):
         at = 2 * (py * NCORE + 1 - core)
         send(("ys", py), yb.at[pl.ds(at, 2)], ys_r.at[py], column(y, 1 - core))
 
-    for d in range(1, NZ):
-        recv("g3", d)
-    tile = p2_r[0]
-    for k in range(1, NZ):
-        tile = tile + p2_r[k]
-    p3_r[pl.ds(core, 1), pl.ds(me, 1)] = tile[None, None, 0:8]
-    p3_r[pl.ds(core, 1), NXY : NXY + 1] = tile[None, None, 8:16]
-    for i, (a, b) in enumerate(xy_steps):
-        o = p3_r.at[core, me]
-        send(("g4", i), o, o, xy_peer(a, b))
-
+    strip = cs[pl.ds(2 * c, 2)].reshape(2 * BLK, 2 * BLK).astype(F32)
+    own_bias = jnp.sum(strip, axis=0, keepdims=True) * SCALE
+    bias_tile = jnp.concatenate(
+        [own_bias[:, :BLK], own_bias[:, BLK:], jnp.zeros((6, BLK), F32)], axis=0
+    )
+
+    rs_a(1)
+    recv("g1", 0)
+    me = x * NY + y
+    for t in range(NZ):
+        p1_s[t, 0:8] = wp[core, 2 * t] + ws_r[2 * t]
+        p1_s[t, 8:16] = wp[core, 2 * t + 1] + ws_r[2 * t + 1]
+        p1_s[t, 16:24] = bias_tile
+    p1_r[pl.ds(z, 1)] = p1_s[pl.ds(z, 1)]
+    for d in (4, 3, 5, 2, 6, 1, 7):
+        send(("g2", d), p1_s.at[zm(d)], p1_r.at[z], plane(x, zm(d)))
+
+    rs_b(0)
     for py in range(NY):
         recv("ys", py)
     for py in range(NY):
@@ -478,43 +518,68 @@
         at = 2 * (ym(d) * NCORE + core)
         send(("yy", d), yb.at[pl.ds(at, 2)], yy_r.at[d - 1], column(ym(d), core))
 
+    rs_a(2)
+    rs_b(1)
+
+    for d in range(1, NZ):
+        recv("g2", d)
+    tile = p1_r[0]
+    for k in range(1, NZ):
+        tile = tile + p1_r[k]
+    p2_r[pl.ds(me, 1)] = tile[None]
+    for i, (a, b) in enumerate(xy_steps):
+        send(("g3", i), p2_r.at[me], p2_r.at[me], xy_peer(a, b))
+
     rs_a(3)
-    rs_rb(2)
-    rs_lb(2)
+    rs_b(2)
 
     own_a = None
-    for f in (1, 2, 3, 0):
+    for f in (2, 1, 3, 0):
         v = ts[t_a(z, xm(f))] + take("ra", 3, f) + take("la", 2, f)
         if f:
             post(("xa", f - 1), v, plane(xm(f), z))
         else:
             own_a = v
-    rs_rb(3)
+    rs_b(3)
     own_b = rs_bg(0) + take("lb", 2)
 
     for i in range(len(xy_steps)):
-        recv("g4", i)
-    o = p3_r.at[core]
-    send(("g5", 0), o, o, column(y, 1 - core))
+        recv("g3", i)
+    tile = p2_r[0]
+    for k in range(1, NXY):
+        tile = tile + p2_r[k]
+    p3_r[pl.ds(core, 1), pl.ds(z, 1)] = tile[None, None, 0:16]
+    p3_r[pl.ds(core, 1), NZ : NZ + 1, 0:8] = tile[None, None, 16:24]
+    p3_r[pl.ds(core, 1), NZ : NZ + 1, 8:16] = jnp.zeros((1, 1, 8, BLK), F32)
+    for d in (4, 3, 5, 2, 6, 1, 7):
+        o = p3_r.at[core, z]
+        send(("g4", d), o, o, plane(x, zm(d)))
 
     for d in range(1, NY):
         recv("yy", d)
     agg = yb[pl.ds(2 * c, 2)]
     for d in range(1, NY):
         agg = agg + yy_r[d - 1]
-    agg_ref[...] = agg.reshape(2 * BLK, BLK)
+    agg_ref[0:BLK] = agg[0].T
+    agg_ref[BLK : 2 * BLK] = agg[1].T
 
     own_b = own_b + take("rb", 3)
     for f in range(1, NX):
         own_a = own_a + take("xa", f - 1)
     gord_ref[0:BLK] = own_a
     gord_ref[BLK : 2 * BLK] = own_b
+
+    for d in range(1, NZ):
+        recv("g4", d)
+    o = p3_r.at[core]
+    send(("g5", 0), o, o, column(y, 1 - core))
+    for d in started[:-1]:
+        d.wait_send()
     recv("g5", 0)
     grads_ref[...] = p3_r[...]
 
     assert not pending, pending.keys()
-    for d in started:
-        d.wait_send()
+    started[-1].wait_send()
 
 
 def final_kernel(agg, gord, grads, nid, weight, bias, out_ref, fg_ref, wg_ref, bg_ref):
@@ -527,8 +592,9 @@
     fg_ref[...] = dot(order, high) + dot(order, low)
     for t in range(2 * NXY):
         a, b = 8 * (t // 2), BLK * (t % 2)
-        wg_ref[a : a + 8, b : b + BLK] = grads[t // NXY, t % NXY]
-    tile = grads[0, NXY] + grads[1, NXY]
+        h, k = t // NXY, t % NXY
+        wg_ref[a : a + 8, b : b + BLK] = grads[h, k // 2, 8 * (k % 2) : 8 * (k % 2) + 8]
+    tile = grads[0, NZ] + grads[1, NZ]
     bg_ref[...] = jnp.concatenate([tile[0:1], tile[1:2]], axis=1)
 
 
@@ -537,17 +603,23 @@
     weight, bias, cotangent,
 ):
     vmem = pl.BlockSpec(memory_space=pltpu.VMEM)
-    smem = pl.BlockSpec(memory_space=pltpu.SMEM)
     tile = (BLK, BLK)
     scratch = [
+        pltpu.VMEM((1, 1), I32),
+        pltpu.VMEM((1, 1, SLOTS), I32),
+        pltpu.VMEM((1, 1, SLOTS), I32),
+        pltpu.VMEM((1, 1, SLOTS), I32),
+        pltpu.VMEM((2 * BLK, BLK), BF16),
+        pltpu.VMEM((1, 2 * BLK), I32),
+        pltpu.VMEM((64, *tile), BF16),
+        pltpu.VMEM((BLK, 2 * BLK), BF16),
         pltpu.VMEM((8, QLEN), I32),
         pltpu.SMEM((8, QLEN), I32),
-        pltpu.VMEM((64, *tile), BF16),
         pltpu.VMEM((2 * NROW + 1, *tile), BF16),
+        pltpu.VMEM((2 * NCOL, BLK, 2 * BLK), BF16),
         pltpu.VMEM((2 * NCOL + 1, BLK, 2 * BLK), BF16),
         pltpu.VMEM((64, *tile), BF16),
-        pltpu.VMEM((2 * BLK, BLK), BF16),
-        pltpu.VMEM((BPAIRS + 1, BLK, 2 * BLK), F32),
+        pltpu.VMEM((BPAIRS + 1, *tile), F32),
         pltpu.VMEM((FPAIRS + 1, *tile), F32),
         pltpu.VMEM((2 * NROW, *tile), F32),
         pltpu.VMEM((2 * NCOL, *tile), F32),
@@ -557,22 +629,22 @@
         pltpu.VMEM((NY - 1, 2, *tile), F32),
         pltpu.VMEM((2, NXY, 8, BLK), F32),
         pltpu.VMEM((NXY, 8, BLK), F32),
-        pltpu.VMEM((NXY, 16, BLK), F32),
-        pltpu.VMEM((NXY, 16, BLK), F32),
-        pltpu.VMEM((NZ, 16, BLK), F32),
-        pltpu.VMEM((2, NXY + 1, 8, BLK), F32),
+        pltpu.VMEM((NZ, 24, BLK), F32),
+        pltpu.VMEM((NZ, 24, BLK), F32),
+        pltpu.VMEM((NXY, 24, BLK), F32),
+        pltpu.VMEM((2, NZ + 1, 16, BLK), F32),
         pltpu.SemaphoreType.DMA((NSEM,)),
         pltpu.SemaphoreType.DMA((NSEM,)),
-        pltpu.SemaphoreType.DMA((2,)),
+        pltpu.SemaphoreType.DMA((10,)),
     ]
     agg, gord, grads = pl.pallas_call(
         main_kernel,
         out_shape=(
             jax.ShapeDtypeStruct((2 * BLK, BLK), F32),
             jax.ShapeDtypeStruct((2 * BLK, BLK), F32),
-            jax.ShapeDtypeStruct((2, NXY + 1, 8, BLK), F32),
+            jax.ShapeDtypeStruct((2, NZ + 1, 16, BLK), F32),
         ),
-        in_specs=[smem] + [vmem] * 5 + [pl.BlockSpec(memory_space=pl.ANY)] + [vmem] * 2,
+        in_specs=[pl.BlockSpec(memory_space=pl.ANY)] * 9,
         out_specs=(vmem,) * 3,
         scratch_shapes=scratch,
         compiler_params=pltpu.CompilerParams(

time: 72.8 us -> 64.6 us (0.89)
  Pallas kernels: 71.4 us -> 63.2 us
    pallas_call x1, Pallas kernels: 69.3 us -> 61.1 us  [body(): pl.pallas_call(main_kernel, out_shape=(jax.ShapeDtypeStruct((2 * BLK, BLK...]
where the time goes in v3:
time: 64.6 us; the launch traced here: 64.5 us
  Pallas kernels  63.2 us (98%)
  between operations  1.29 us (2%)
    pallas_call x1, Pallas kernels, body(): pl.pallas_call(main_kernel, out_shape=(jax.ShapeDtypeStruct((2 * BLK, BLK...  61.1 us
    pallas_call x1, Pallas kernels, body(): pl.pallas_call(final_kernel, out_shape=(jax.ShapeDtypeStruct((2 * BLK, 2...  2.14 us

profile of v3, /device:TPU:1, one launch (start us, length us, event | category | flops | bytes accessed | tf_op | source)
XLA Modules:
  0.0 64.5 jit_solution(7225347057655392224)
XLA Ops:
  1.3 61.1 %shard_map.129 = (f32[256,128]{1,0:T(8,128)}, f32[256,128]{1,0:T(8,128)}, f32[2,9,16,128]{3,2,1,0:T(8,128)}) custom-call(s32[1,1]{1,0:T(1,128)S(6)} %copy.14.live_h, s32[1,1,256]{2,1,0:T(1,128)} %rows_h.1, s32[1,1,256]{2,1,0:T(1,128)} %cols_h.1, s32[1,1,256]{2,1,0:T(1,128)} %ids_h.1, bf16[256,128]{1,0:T(8,128)(2,1)} %feat_h.1, s32[1,256]{1,0:T(1,128)} %nid.1, ...), custom_call_target="tpu_custom_call" | custom-call | tf_op jit(solution)/shard_map/pallas_call | solution.py:640
  62.3 2.1 %shard_map.130 = (f32[256,256]{1,0:T(8,128)}, f32[256,128]{1,0:T(8,128)}, f32[128,256]{1,0:T(8,128)}, f32[1,256]{1,0:T(1,128)}) custom-call(f32[256,128]{1,0:T(8,128)} %get-tuple-element.11.agg, f32[256,128]{1,0:T(8,128)} %get-tuple-element.12.gord, f32[2,9,16,128]{3,2,1,0:T(8,128)} %get-tuple-element.13.grads, s32[1,256]{1,0:T(1,128)} %nid.1, ...), custom_call_target="tpu_custom_call" | custom-call | tf_op jit(solution)/shard_map/pallas_call | solution.py:657

commit v4 on v3

--- a/solution.py
+++ b/solution.py
@@ -141,9 +141,9 @@
 
 
 def main_kernel(
-    live_h, rows_h, cols_h, ids_h, feat_h, nid_h, edge_h, weight_h, cot_h,
-    agg_ref, gord_ref, grads_ref,
-    live, rows, cols, ids, feat, nid, edge, weight,
+    live_h, rows_h, cols_h, ids_h, feat_h, nid_h, edge_h, weight_h, cot_h, bias_h,
+    out_h, fg_h, wg_h, bg_h,
+    live, rows, cols, ids, feat, nid, edge, weight, bias, out_v, fg_v, wg_v, bg_v,
     plan_v, idx, xs, cs, phl, et, sb, sf, ts, yb, sbuf, rbuf, ys_r, yy_r,
     wp, ws_r, p1_s, p1_r, p2_r, p3_r, ss, rs, ls,
 ):
@@ -186,10 +186,17 @@
     def recv(*key):
         pending.pop(key).wait_recv()
 
+    stores = []
+
+    def store(src, dst):
+        d = pltpu.make_async_copy(src, dst, ls.at[len(loads) + 1 + len(stores)])
+        d.start()
+        stores.append(d)
+
     xy_steps = [(a, b) for a in range(NX) for b in range(NY) if a or b]
 
     barrier = pltpu.get_barrier_semaphore()
-    peers = [plane(x, zm(1)), plane(x, zm(-1))]
+    peers = [plane(x, zm(d)) for d in (2, -2, 1, -1)]
     peers += [plane(xm(d), z) for d in range(1, NX)]
     peers += [column(ym(d), core) for d in range(1, NY)]
     peers += [column(y, 1 - core)]
@@ -200,7 +207,7 @@
         ("feat", feat_h, feat), ("nid", nid_h, nid),
         ("cot", cot_h, cs.at[pl.ds(2 * c, 2)]), ("rows", rows_h, rows), ("cols", cols_h, cols),
         ("ids", ids_h, ids), ("live", live_h, live), ("weight", weight_h, weight),
-        ("edge", edge_h, edge),
+        ("edge", edge_h, edge), ("bias", bias_h, bias),
     ]):
         loads[name] = pltpu.make_async_copy(src, dst, ls.at[k])
         loads[name].start()
@@ -211,11 +218,6 @@
     ordered = dot(feat[...].T, order.astype(BF16)).astype(BF16)
     xs[pl.ds(z * NX + x, 1)] = ordered[None, :, :BLK]
     xs[pl.ds(NROW + r, 1)] = ordered[None, :, BLK:]
-    for name in ("rows", "cols", "ids", "live"):
-        loads[name].wait()
-    plan_slots(rows, cols, ids, live, plan_v)
-    plan_copy = pltpu.make_async_copy(plan_v, idx, ls.at[len(loads)])
-    plan_copy.start()
     loads["cot"].wait()
     pl.semaphore_wait(barrier, len(peers))
 
@@ -225,17 +227,19 @@
     def b_at(px, pz):
         return xs.at[NROW + px * NZ + pz]
 
+    side = (1, 1, -1, -1)
+
     def ag_ar(s, f):
-        o = a_at(zm(1 - s), xm(-f))
-        send(("ar", s, f), o, o, plane(x, zm(1)))
+        o = a_at(zm(side[f] * (-2 if s == 4 else 1 - s)), xm(-f))
+        send(("ar", s, f), o, o, plane(x, zm(side[f] * (2 if s == 4 else 1))))
 
     def ag_al(s, f):
-        o = a_at(zm(s - 1), xm(-f))
-        send(("al", s, f), o, o, plane(x, zm(-1)))
+        o = a_at(zm(side[f] * (s - 1)), xm(-f))
+        send(("al", s, f), o, o, plane(x, zm(-side[f])))
 
     def ag_br(s):
-        o = b_at(x, zm(1 - s))
-        send(("br", s), o, o, plane(x, zm(1)))
+        o = b_at(x, zm(-2 if s == 4 else 1 - s))
+        send(("br", s), o, o, plane(x, zm(2 if s == 4 else 1)))
 
     def ag_bl(s):
         o = b_at(x, zm(s - 1))
@@ -262,6 +266,11 @@
         send(("cs", 0, h), o, o, column(y, 1 - core))
     ag_bx(0)
 
+    for name in ("rows", "cols", "ids", "live"):
+        loads[name].wait()
+    plan_slots(rows, cols, ids, live, plan_v)
+    plan_copy = pltpu.make_async_copy(plan_v, idx, ls.at[len(loads)])
+    plan_copy.start()
     xs[2 * NROW] = jnp.zeros((BLK, BLK), BF16)
     phl[2 * NCOL] = jnp.zeros((BLK, 2 * BLK), BF16)
     sb[BPAIRS] = jnp.zeros((BLK, BLK), F32)
@@ -269,8 +278,11 @@
 
     def ag_b(s):
         recv("br", s)
+        if s == 2:
+            ag_br(4)
+        if s < 3:
+            ag_br(s + 1)
         if s < 4:
-            ag_br(s + 1)
             recv("bl", s)
             if s < 3:
                 ag_bl(s + 1)
@@ -281,8 +293,11 @@
     def ag_a(s, flows=(0, 1, 3, 2)):
         for f in flows:
             recv("ar", s, f)
+            if s == 2:
+                ag_ar(4, f)
+            if s < 3:
+                ag_ar(s + 1, f)
             if s < 4:
-                ag_ar(s + 1, f)
                 recv("al", s, f)
                 if s < 3:
                     ag_al(s + 1, f)
@@ -297,6 +312,7 @@
     ag_a(1, (1, 3, 2))
     ag_a(2, (0,))
     loads["weight"].wait()
+    loads["bias"].wait()
     loads["edge"].wait()
 
     def turn(k, carry):
@@ -324,6 +340,7 @@
         project(ym(d) * NCORE + core)
     ag_b(3)
     ag_a(2, (1, 3, 2))
+    ag_b(4)
     for h in range(2):
         for d in range(NY):
             recv("cs", d, h)
@@ -364,10 +381,7 @@
     forth = pair(0, True, sf)
 
     zero = jnp.zeros((BLK, BLK), F32)
-    total = run_pairs(0, 80, 20, zero, back)
-    ag_b(4)
-    ag_a(3)
-    run_pairs(80, 160, 20, total, back)
+    run_pairs(0, 160, 40, zero, back)
 
     def stage(k, carry):
         for u in range(8):
@@ -394,8 +408,8 @@
         pending[key] = d
         started.append(d)
 
-    b_order = (4, 5, 3, 6, 2, 7, 1, 0)
-    b_groups = ((0, 2), (2, 4), (4, 6), (6, 8))
+    b_order = (4, 3, 5, 2, 6, 1, 7, 0)
+    b_groups = ((0, 3), (3, 5), (5, 8))
 
     def rs_bx(g):
         lo, hi = b_groups[g]
@@ -425,63 +439,72 @@
         recv(*key)
         return decode(rbuf.at[SEM[key[0]](*key[1:])])
 
+    def got(*key):
+        return decode(rbuf.at[SEM[key[0]](*key[1:])])
+
     def rs_a(s):
-        for f in range(NX):
-            v = ts[t_a(zm(4 - s), xm(f))]
-            if s:
-                v = v + take("ra", s - 1, f)
-            post(("ra", s, f), v, plane(x, zm(1)))
-            if s < 3:
-                v = ts[t_a(zm(s - 3), xm(f))]
-                if s:
-                    v = v + take("la", s - 1, f)
-                post(("la", s, f), v, plane(x, zm(-1)))
-
-    def rs_rb(s):
-        v = rs_bg((4 - s) % NZ)
-        if s:
-            v = v + take("rb", s - 1)
-        post(("rb", s), v, plane(x, zm(1)))
-
-    def rs_lb(s):
-        v = rs_bg((s - 3) % NZ)
-        if s:
-            v = v + take("lb", s - 1)
-        post(("lb", s), v, plane(x, zm(-1)))
+        for f in (2, 0, 3, 1):
+            d = side[f]
+            up, up_two, down = plane(x, zm(d)), plane(x, zm(2 * d)), plane(x, zm(-d))
+
+            def own(k):
+                return ts[t_a(zm(d * k), xm(f))]
+
+            if s == 0:
+                first = [(("ra", 0, f), 4, up_two), (("ra", 1, f), 3, up), (("la", 0, f), -3, down)]
+                for key, k, _ in first:
+                    encode(own(k), sbuf.at[SEM[key[0]](*key[1:])])
+                for key, _, dev in first:
+                    k = SEM[key[0]](*key[1:])
+                    send(key, sbuf.at[k], rbuf.at[k], dev)
+            elif s == 1:
+                recv("ra", 1, f)
+                recv("ra", 0, f)
+                post(("ra", 2, f), own(2) + got("ra", 0, f) + got("ra", 1, f), up)
+                post(("la", 1, f), own(-2) + take("la", 0, f), down)
+            else:
+                post(("ra", 3, f), own(1) + take("ra", 2, f), up)
+                post(("la", 2, f), own(-1) + take("la", 1, f), down)
 
     def rs_b(s):
+        up, up_two, down = plane(x, zm(1)), plane(x, zm(2)), plane(x, zm(-1))
         rs_bx_recv(s)
-        rs_rb(s)
-        if s < 3:
-            rs_lb(s)
+        if s == 0:
+            post(("rb", 0), rs_bg(4), up_two)
+            post(("rb", 1), rs_bg(3), up)
+            post(("lb", 0), rs_bg(5), down)
+        elif s == 1:
+            recv("rb", 1)
+            recv("rb", 0)
+            post(("rb", 2), rs_bg(2) + got("rb", 0) + got("rb", 1), up)
+            post(("lb", 1), rs_bg(6) + take("lb", 0), down)
+        else:
+            post(("rb", 3), rs_bg(1) + take("rb", 2), up)
+            post(("lb", 2), rs_bg(7) + take("lb", 1), down)
 
     rs_bx(0)
     rs_a(0)
-    for g in (1, 2, 3):
-        rs_bx(g)
-
+    rs_bx(1)
+    rs_bx(2)
+
+    ag_a(3)
     ag_a(4)
     for rel in (0, 1, 7, 2, 6, 3, 5, 4):
         for d in range(1, NX):
             recv("bx", rel, d)
 
-    run_pairs(0, 136, 17, zero, forth)
-
-    def stage_y(k, carry):
-        for u in range(4):
-            yb[4 * k + u] = sf[idx[6, 4 * k + u]]
-        return carry
-
-    lax.fori_loop(0, 2 * NCOL // 4, stage_y, 0)
-    def grad(k, acc):
-        for u in range(2):
-            at = 4 * k + 2 * u
-            strip = cs[pl.ds(at, 2)].reshape(2 * BLK, 2 * BLK)
-            high, low = split(jnp.concatenate([yb[at], yb[at + 1]], axis=1))
-            acc = acc + dot(high, strip) + dot(low, strip)
-        return acc
-
-    acc = lax.fori_loop(0, NCOL // 2, grad, jnp.zeros((BLK, 2 * BLK), F32)) * SCALE
+    run_pairs(0, 136, 34, zero, forth)
+
+    acc = None
+    for at in range(0, 2 * NCOL, 2):
+        strip = cs[at : at + 2].reshape(2 * BLK, 2 * BLK)
+        wide = jnp.concatenate([sf[idx[6, at]], sf[idx[6, at + 1]]], axis=1)
+        yb[at] = wide[:, :BLK]
+        yb[at + 1] = wide[:, BLK:]
+        high, low = split(wide)
+        part = dot(high, strip) + dot(low, strip)
+        acc = part if acc is None else acc + part
+    acc = acc * SCALE
     for t in range(2 * NXY):
         a, b = 8 * (t // 2), BLK * (t % 2)
         wp[t // NXY, t % NXY] = acc[a : a + 8, b : b + BLK]
@@ -497,7 +520,6 @@
         [own_bias[:, :BLK], own_bias[:, BLK:], jnp.zeros((6, BLK), F32)], axis=0
     )
 
-    rs_a(1)
     recv("g1", 0)
     me = x * NY + y
     for t in range(NZ):
@@ -509,6 +531,7 @@
         send(("g2", d), p1_s.at[zm(d)], p1_r.at[z], plane(x, zm(d)))
 
     rs_b(0)
+    rs_a(1)
     for py in range(NY):
         recv("ys", py)
     for py in range(NY):
@@ -518,9 +541,6 @@
         at = 2 * (ym(d) * NCORE + core)
         send(("yy", d), yb.at[pl.ds(at, 2)], yy_r.at[d - 1], column(ym(d), core))
 
-    rs_a(2)
-    rs_b(1)
-
     for d in range(1, NZ):
         recv("g2", d)
     tile = p1_r[0]
@@ -530,18 +550,8 @@
     for i, (a, b) in enumerate(xy_steps):
         send(("g3", i), p2_r.at[me], p2_r.at[me], xy_peer(a, b))
 
-    rs_a(3)
-    rs_b(2)
-
-    own_a = None
-    for f in (2, 1, 3, 0):
-        v = ts[t_a(z, xm(f))] + take("ra", 3, f) + take("la", 2, f)
-        if f:
-            post(("xa", f - 1), v, plane(xm(f), z))
-        else:
-            own_a = v
-    rs_b(3)
-    own_b = rs_bg(0) + take("lb", 2)
+    rs_b(1)
+    rs_a(2)
 
     for i in range(len(xy_steps)):
         recv("g3", i)
@@ -555,54 +565,72 @@
         o = p3_r.at[core, z]
         send(("g4", d), o, o, plane(x, zm(d)))
 
+    while started:
+        started.pop(0).wait_send()
+    rs_b(2)
+    own_a = None
+    for f in (2, 1, 3, 0):
+        v = ts[t_a(z, xm(f))] + take("ra", 3, f) + take("la", 2, f)
+        if f:
+            post(("xa", f - 1), v, plane(xm(f), z))
+        else:
+            own_a = v
+    own_b = rs_bg(0)
+
     for d in range(1, NY):
         recv("yy", d)
     agg = yb[pl.ds(2 * c, 2)]
     for d in range(1, NY):
         agg = agg + yy_r[d - 1]
-    agg_ref[0:BLK] = agg[0].T
-    agg_ref[BLK : 2 * BLK] = agg[1].T
-
-    own_b = own_b + take("rb", 3)
+    high, low = split(jnp.concatenate([agg[0].T, agg[1].T], axis=0))
+    out_v[...] = dot(high, weight[...]) + dot(low, weight[...]) + bias[...]
+    store(out_v, out_h)
+
+    own_b = own_b + take("rb", 3) + take("lb", 2)
     for f in range(1, NX):
         own_a = own_a + take("xa", f - 1)
-    gord_ref[0:BLK] = own_a
-    gord_ref[BLK : 2 * BLK] = own_b
+    high, low = split(jnp.concatenate([own_a, own_b], axis=0))
+    fg_v[...] = dot(order.astype(BF16), high) + dot(order.astype(BF16), low)
+    store(fg_v, fg_h)
 
     for d in range(1, NZ):
         recv("g4", d)
     o = p3_r.at[core]
     send(("g5", 0), o, o, column(y, 1 - core))
-    for d in started[:-1]:
-        d.wait_send()
     recv("g5", 0)
-    grads_ref[...] = p3_r[...]
-
-    assert not pending, pending.keys()
-    started[-1].wait_send()
-
-
-def final_kernel(agg, gord, grads, nid, weight, bias, out_ref, fg_ref, wg_ref, bg_ref):
-    high, low = split(agg[...])
-    out_ref[...] = dot(high, weight[...]) + dot(low, weight[...]) + bias[...]
-    order = jnp.where(
-        lax.broadcasted_iota(jnp.int32, (2 * BLK, 2 * BLK), 0) == nid[...], 1.0, 0.0
-    ).astype(BF16)
-    high, low = split(gord[...])
-    fg_ref[...] = dot(order, high) + dot(order, low)
     for t in range(2 * NXY):
         a, b = 8 * (t // 2), BLK * (t % 2)
         h, k = t // NXY, t % NXY
-        wg_ref[a : a + 8, b : b + BLK] = grads[h, k // 2, 8 * (k % 2) : 8 * (k % 2) + 8]
-    tile = grads[0, NZ] + grads[1, NZ]
-    bg_ref[...] = jnp.concatenate([tile[0:1], tile[1:2]], axis=1)
+        wg_v[a : a + 8, b : b + BLK] = p3_r[h, k // 2, 8 * (k % 2) : 8 * (k % 2) + 8]
+    tile = p3_r[0, NZ] + p3_r[1, NZ]
+    bg_v[...] = jnp.concatenate([tile[0:1], tile[1:2]], axis=1)
+    store(wg_v, wg_h)
+    store(bg_v, bg_h)
+
+    assert not pending, pending.keys()
+    for d in started:
+        d.wait_send()
+    for d in stores:
+        d.wait()
+
+
+def copy_kernel(out_s, fg_s, wg_s, bg_s, out_h, fg_h, wg_h, bg_h, out_v, fg_v, wg_v, bg_v, sems):
+    hops = [(wg_s, wg_v, wg_h), (out_s, out_v, out_h), (fg_s, fg_v, fg_h), (bg_s, bg_v, bg_h)]
+    loads = [pltpu.make_async_copy(a, b, sems.at[k]) for k, (a, b, _) in enumerate(hops)]
+    stores = [pltpu.make_async_copy(b, c, sems.at[4 + k]) for k, (_, b, c) in enumerate(hops)]
+    for d in loads:
+        d.start()
+    for load, store in zip(loads, stores):
+        load.wait()
+        store.start()
+    for d in stores:
+        d.wait()
 
 
 def body(
     features, node_ids, edge_blocks, block_rows, block_cols, block_ids, live_blocks,
     weight, bias, cotangent,
 ):
-    vmem = pl.BlockSpec(memory_space=pltpu.VMEM)
     tile = (BLK, BLK)
     scratch = [
         pltpu.VMEM((1, 1), I32),
@@ -613,6 +641,11 @@
         pltpu.VMEM((1, 2 * BLK), I32),
         pltpu.VMEM((64, *tile), BF16),
         pltpu.VMEM((BLK, 2 * BLK), BF16),
+        pltpu.VMEM((1, 2 * BLK), F32),
+        pltpu.VMEM((2 * BLK, 2 * BLK), F32),
+        pltpu.VMEM((2 * BLK, BLK), F32),
+        pltpu.VMEM((BLK, 2 * BLK), F32),
+        pltpu.VMEM((1, 2 * BLK), F32),
         pltpu.VMEM((8, QLEN), I32),
         pltpu.SMEM((8, QLEN), I32),
         pltpu.VMEM((2 * NROW + 1, *tile), BF16),
@@ -635,36 +668,35 @@
         pltpu.VMEM((2, NZ + 1, 16, BLK), F32),
         pltpu.SemaphoreType.DMA((NSEM,)),
         pltpu.SemaphoreType.DMA((NSEM,)),
-        pltpu.SemaphoreType.DMA((10,)),
+        pltpu.SemaphoreType.DMA((15,)),
     ]
-    agg, gord, grads = pl.pallas_call(
+    shapes = (
+        jax.ShapeDtypeStruct((2 * BLK, 2 * BLK), F32),
+        jax.ShapeDtypeStruct((2 * BLK, BLK), F32),
+        jax.ShapeDtypeStruct((BLK, 2 * BLK), F32),
+        jax.ShapeDtypeStruct((1, 2 * BLK), F32),
+    )
+    anywhere = pl.BlockSpec(memory_space=pl.ANY)
+    results = pl.pallas_call(
         main_kernel,
-        out_shape=(
-            jax.ShapeDtypeStruct((2 * BLK, BLK), F32),
-            jax.ShapeDtypeStruct((2 * BLK, BLK), F32),
-            jax.ShapeDtypeStruct((2, NZ + 1, 16, BLK), F32),
-        ),
-        in_specs=[pl.BlockSpec(memory_space=pl.ANY)] * 9,
-        out_specs=(vmem,) * 3,
+        out_shape=shapes,
+        in_specs=[anywhere] * 10,
+        out_specs=(anywhere,) * 4,
         scratch_shapes=scratch,
         compiler_params=pltpu.CompilerParams(
             collective_id=0, has_side_effects=True, vmem_limit_bytes=58 * 2**20
         ),
     )(
         live_blocks, block_rows, block_cols, block_ids, features, node_ids, edge_blocks,
-        weight, cotangent.reshape(2, BLK, 2 * BLK),
+        weight, cotangent.reshape(2, BLK, 2 * BLK), bias.reshape(1, -1),
     )
     layer_out, feature_grad, weight_grad, bias_grad = pl.pallas_call(
-        final_kernel,
-        out_shape=(
-            jax.ShapeDtypeStruct((2 * BLK, 2 * BLK), F32),
-            jax.ShapeDtypeStruct((2 * BLK, BLK), F32),
-            jax.ShapeDtypeStruct((BLK, 2 * BLK), F32),
-            jax.ShapeDtypeStruct((1, 2 * BLK), F32),
-        ),
-        in_specs=[vmem] * 6,
-        out_specs=(vmem,) * 4,
-    )(agg, gord, grads, node_ids, weight, bias.reshape(1, -1))
+        copy_kernel,
+        out_shape=shapes,
+        in_specs=[anywhere] * 4,
+        out_specs=(anywhere,) * 4,
+        scratch_shapes=[pltpu.VMEM(t.shape, F32) for t in shapes] + [pltpu.SemaphoreType.DMA((8,))],
+    )(*results)
     return layer_out, feature_grad, weight_grad, bias_grad.reshape(-1)
 
 

time: 64.6 us -> 61.8 us (0.957)
  Pallas kernels: 63.2 us -> 60.3 us
    pallas_call x2, Pallas kernels: 63.2 us -> 60.3 us  [the longest x1 58.5 us: body(): pl.pallas_call(main_kernel, out_shape=shapes, in_specs=[anywhere] * 10, o...]
where the time goes in v4:
time: 61.8 us; the launch traced here: 61.6 us
  Pallas kernels  60.3 us (98%)
  between operations  1.29 us (2%)
    pallas_call x1, Pallas kernels, body(): pl.pallas_call(main_kernel, out_shape=shapes, in_specs=[anywhere] * 10, o...  58.5 us
    pallas_call x1, Pallas kernels, body(): pl.pallas_call(copy_kernel, out_shape=shapes, in_specs=[anywhere] * 4, ou...  1.83 us

profile of v4, /device:TPU:1, one launch (start us, length us, event | category | flops | bytes accessed | tf_op | source)
XLA Modules:
  0.0 61.6 jit_solution(743907323198648130)
XLA Ops:
  1.3 58.5 %shard_map.129 = (f32[256,256]{1,0:T(8,128)}, f32[256,128]{1,0:T(8,128)}, f32[128,256]{1,0:T(8,128)}, f32[1,256]{1,0:T(1,128)}) custom-call(s32[1,1]{1,0:T(1,128)S(6)} %copy.14.live_h, s32[1,1,256]{2,1,0:T(1,128)} %rows_h.1, s32[1,1,256]{2,1,0:T(1,128)} %cols_h.1, s32[1,1,256]{2,1,0:T(1,128)} %ids_h.1, bf16[256,128]{1,0:T(8,128)(2,1)} %feat_h.1, ...), custom_call_target="tpu_custom_call" | custom-call | tf_op jit(solution)/shard_map/pallas_call | solution.py:680
  59.8 1.8 %shard_map.130 = (f32[256,256]{1,0:T(8,128)}, f32[256,128]{1,0:T(8,128)}, f32[128,256]{1,0:T(8,128)}, f32[1,256]{1,0:T(1,128)}) custom-call(f32[256,256]{1,0:T(8,128)} %get-tuple-element.12.out_s, f32[256,128]{1,0:T(8,128)} %get-tuple-element.13.fg_s, f32[128,256]{1,0:T(8,128)} %get-tuple-element.14.wg_s, f32[1,256]{1,0:T(1,128)} %get-tuple-element.15.bg_s), custom_call_target="tpu_custom_call" | custom-call | tf_op jit(solution)/shard_map/pallas_call | solution.py:693

commit v5 on v4

--- a/solution.py
+++ b/solution.py
@@ -144,7 +144,7 @@
     live_h, rows_h, cols_h, ids_h, feat_h, nid_h, edge_h, weight_h, cot_h, bias_h,
     out_h, fg_h, wg_h, bg_h,
     live, rows, cols, ids, feat, nid, edge, weight, bias, out_v, fg_v, wg_v, bg_v,
-    plan_v, idx, xs, cs, phl, et, sb, sf, ts, yb, sbuf, rbuf, ys_r, yy_r,
+    plan_v, idx, xs, cs, phl, et, sb, sf, yb, sbuf, rbuf, ys_r, yy_r,
     wp, ws_r, p1_s, p1_r, p2_r, p3_r, ss, rs, ls,
 ):
     r = lax.axis_index("row")
@@ -250,6 +250,10 @@
         for d in (2, 1, 3):
             send(("bx", rel, d), o, o, plane(xm(d), z))
 
+    for h in range(2):
+        o = cs.at[2 * c + h]
+        for d in (2, 1, 3):
+            send(("cy", d, h), o, o, column(ym(d), core))
     own = a_at(z, x)
     ag_br(1)
     ag_bl(1)
@@ -257,10 +261,6 @@
         send(("ax", d), own, own, plane(xm(d), z))
     ag_ar(1, 0)
     ag_al(1, 0)
-    for h in range(2):
-        o = cs.at[2 * c + h]
-        for d in (2, 1, 3):
-            send(("cy", d, h), o, o, column(ym(d), core))
     for h in range(2):
         o = cs.at[2 * c + h]
         send(("cs", 0, h), o, o, column(y, 1 - core))
@@ -383,12 +383,8 @@
     zero = jnp.zeros((BLK, BLK), F32)
     run_pairs(0, 160, 40, zero, back)
 
-    def stage(k, carry):
-        for u in range(8):
-            ts[8 * k + u] = sb[idx[7, 8 * k + u]]
-        return carry
-
-    lax.fori_loop(0, 2 * NROW // 8, stage, 0)
+    def product(at):
+        return sb[idx[7, at]]
 
     def t_a(pz, px):
         return pz * NX + px
@@ -397,7 +393,7 @@
         return NROW + px * NZ + pz
 
     def b_value(px, pz):
-        return ts[t_b(px, pz)]
+        return product(t_b(px, pz))
 
     def send_many(key, k, src, dst, dev):
         d = pltpu.make_async_remote_copy(
@@ -448,7 +444,7 @@
             up, up_two, down = plane(x, zm(d)), plane(x, zm(2 * d)), plane(x, zm(-d))
 
             def own(k):
-                return ts[t_a(zm(d * k), xm(f))]
+                return product(t_a(zm(d * k), xm(f)))
 
             if s == 0:
                 first = [(("ra", 0, f), 4, up_two), (("ra", 1, f), 3, up), (("la", 0, f), -3, down)]
@@ -482,10 +478,9 @@
             post(("rb", 3), rs_bg(1) + take("rb", 2), up)
             post(("lb", 2), rs_bg(7) + take("lb", 1), down)
 
+    rs_a(0)
     rs_bx(0)
-    rs_a(0)
     rs_bx(1)
-    rs_bx(2)
 
     ag_a(3)
     ag_a(4)
@@ -530,6 +525,7 @@
     for d in (4, 3, 5, 2, 6, 1, 7):
         send(("g2", d), p1_s.at[zm(d)], p1_r.at[z], plane(x, zm(d)))
 
+    rs_bx(2)
     rs_b(0)
     rs_a(1)
     for py in range(NY):
@@ -570,7 +566,7 @@
     rs_b(2)
     own_a = None
     for f in (2, 1, 3, 0):
-        v = ts[t_a(z, xm(f))] + take("ra", 3, f) + take("la", 2, f)
+        v = product(t_a(z, xm(f))) + take("ra", 3, f) + take("la", 2, f)
         if f:
             post(("xa", f - 1), v, plane(xm(f), z))
         else:
@@ -654,7 +650,6 @@
         pltpu.VMEM((64, *tile), BF16),
         pltpu.VMEM((BPAIRS + 1, *tile), F32),
         pltpu.VMEM((FPAIRS + 1, *tile), F32),
-        pltpu.VMEM((2 * NROW, *tile), F32),
         pltpu.VMEM((2 * NCOL, *tile), F32),
         pltpu.VMEM((NCODED, MSG, BLK), I16),
         pltpu.VMEM((NCODED, MSG, BLK), I16),

time: 61.8 us -> 60.7 us (0.982)
  Pallas kernels: 60.3 us -> 59.3 us
    pallas_call x1, Pallas kernels: 58.5 us -> 57.4 us  [body(): pl.pallas_call(main_kernel, out_shape=shapes, in_specs=[anywhere] * 10, o...]
where the time goes in v5:
time: 60.7 us; the launch traced here: 60.6 us
  Pallas kernels  59.3 us (98%)
  between operations  1.29 us (2%)
    pallas_call x1, Pallas kernels, body(): pl.pallas_call(main_kernel, out_shape=shapes, in_specs=[anywhere] * 10, o...  57.4 us
    pallas_call x1, Pallas kernels, body(): pl.pallas_call(copy_kernel, out_shape=shapes, in_specs=[anywhere] * 4, ou...  1.83 us

profile of v5, /device:TPU:1, one launch (start us, length us, event | category | flops | bytes accessed | tf_op | source)
XLA Modules:
  0.0 60.6 jit_solution(1423484012820098736)
XLA Ops:
  1.3 57.4 %shard_map.129 = (f32[256,256]{1,0:T(8,128)}, f32[256,128]{1,0:T(8,128)}, f32[128,256]{1,0:T(8,128)}, f32[1,256]{1,0:T(1,128)}) custom-call(s32[1,1]{1,0:T(1,128)S(6)} %copy.14.live_h, s32[1,1,256]{2,1,0:T(1,128)} %rows_h.1, s32[1,1,256]{2,1,0:T(1,128)} %cols_h.1, s32[1,1,256]{2,1,0:T(1,128)} %ids_h.1, bf16[256,128]{1,0:T(8,128)(2,1)} %feat_h.1, ...), custom_call_target="tpu_custom_call" | custom-call | tf_op jit(solution)/shard_map/pallas_call | solution.py:675
  58.7 1.8 %shard_map.130 = (f32[256,256]{1,0:T(8,128)}, f32[256,128]{1,0:T(8,128)}, f32[128,256]{1,0:T(8,128)}, f32[1,256]{1,0:T(1,128)}) custom-call(f32[256,256]{1,0:T(8,128)} %get-tuple-element.12.out_s, f32[256,128]{1,0:T(8,128)} %get-tuple-element.13.fg_s, f32[128,256]{1,0:T(8,128)} %get-tuple-element.14.wg_s, f32[1,256]{1,0:T(1,128)} %get-tuple-element.15.bg_s), custom_call_target="tpu_custom_call" | custom-call | tf_op jit(solution)/shard_map/pallas_call | solution.py:688
